TPU v7x, 128 devices: a whole 4x4x4 slice. The times are simulated.
128 devices in a mesh: point: 16 (over x, z), cent: 8 (over y, core).
Axes of the slice: x: 4, y: 4, z: 4, core: 2. Of those that a mesh axis runs over, the one named last changes fastest.
Arguments:
- points: bfloat16 [65536, 1024], P(('point', 'cent')), may hold values from -0.1875 to 0.1875
- assign: int32 [65536], P(('point', 'cent')), may hold values from 0 to 8191
- old_centroids: bfloat16 [8192, 1024], P('cent'), may hold values from -0.1875 to 0.1875
Outputs:
- new_centroids: bfloat16 [8192, 1024], P('cent')
- distances: float32 [65536, 8192], P('point', 'cent')
All inputs are finite; a program needn't handle non-finite values.
Results may differ from a plain program's by a relative error of at most 0.008.
Values may be sent and summed in bfloat16 or wider, within the bound.
A program may use at most 128 MiB of HBM per device.

v0:
```python
import jax
import jax.numpy as jnp
from jax import lax
from jax.sharding import PartitionSpec as P


def finish_rows(totals, counts, old_rows):
    old_wide = old_rows.astype(jnp.float32)
    mean_rows = totals / jnp.maximum(counts, 1.0)[:, None]
    blended = jnp.where((counts > 0.0)[:, None], 0.5 * mean_rows + 0.5 * old_wide, old_wide)
    scaling = lax.rsqrt(jnp.sum(blended * blended, axis=1) + 1e-06)
    return (blended * scaling[:, None]).astype(jnp.bfloat16)


def shards(points, assign, old_centroids):
    owned_rows = old_centroids.shape[0]
    group_points, group_labels = (
        lax.all_gather(points, "cent", axis=0, tiled=True),
        lax.all_gather(assign, "cent", axis=0, tiled=True),
    )
    block_ids = lax.axis_index("cent") * owned_rows + jnp.arange(owned_rows, dtype=jnp.int32)
    onehot = (block_ids[:, None] == group_labels[None, :]).astype(jnp.bfloat16)
    partial_rows = jnp.dot(onehot, group_points, preferred_element_type=jnp.float32)
    partial_counts = jnp.sum(onehot, axis=1, dtype=jnp.float32)
    totals, counts = (
        lax.psum(partial_rows.astype(jnp.bfloat16), "point").astype(jnp.float32),
        lax.psum(partial_counts.astype(jnp.bfloat16), "point").astype(jnp.float32),
    )
    new_centroids = finish_rows(totals, counts, old_centroids)
    cent_sq = jnp.sum(jnp.square(new_centroids.astype(jnp.float32)), axis=1)
    products = lax.dot_general(
        group_points, new_centroids, (((1,), (1,)), ((), ())), preferred_element_type=jnp.float32
    )
    point_sq = jnp.sum(jnp.square(group_points.astype(jnp.float32)), axis=1)
    distances = point_sq[:, None] + cent_sq[None, :] - 2.0 * products
    return (new_centroids, distances)


def solution(mesh):
    return jax.shard_map(
        shards,
        mesh=mesh,
        in_specs=(P(("point", "cent"), None), P(("point", "cent")), P("cent", None)),
        out_specs=(P("cent", None), P("point", "cent")),
        check_vma=False,
    )
```

profile of v0, /device:TPU:0, one launch (start us, length us, event | category | flops | bytes accessed | tf_op | source)
XLA Modules:
  0.0 211.4 jit_solution(14868169910710616072)
XLA Ops:
  7.2 0.0 all-gather.3.cloned.1.call-start
  7.2 0.7 all-gather.3.cloned.1.call-update
  7.9 0.0 all-reduce.2.cloned.1.call-start
  7.9 12.3 %all-gather = s32[8,1,512]{2,1,0:T(1,128)S(1)} all-gather(s32[1,1,512]{2,1,0:T(1,128)} %bitcast.9), channel_id=1, replica_groups=mesh['point'=16,'cent'=8] {'cent'}, dimensions={0}, use_global_device_ids=true | all-gather | bytes 18432 | tf_op jit(solution)/shard_map/all_gather | solution.py:19
  20.3 41.7 %all-gather.3.cloned.1.call-done = bf16[4096,1024]{1,0:T(8,128)(2,1)} async-done(((bf16[512,1024]{1,0:T(8,128)(2,1)}), bf16[4096,1024]{1,0:T(8,128)(2,1)}) %all-gather.3.cloned.1.call-update) | async-done | bytes 8388624 | tf_op jit(solution)/shard_map/all_gather | solution.py:18
  61.9 13.5 %fusion.6 = bf16[1024,1024]{1,0:T(8,128)(2,1)} fusion(bf16[4096,1024]{1,0:T(8,128)(2,1)} %all-gather.3.cloned.1.call-done, s32[4096]{0:T(1024)S(1)} %bitcast.7, s32[1024]{0:T(1024)S(1)} %iota_add_fusion), kind=kOutput, calls=%fused_computation.14 | convolution fusion | flops 8595177472 | bytes 10506240 | tf_op jit(solution)/shard_map/dot_general | solution.py:23
  75.5 0.0 all-reduce.2.cloned.1.call-update
  75.5 1.9 fusion.2
  77.4 40.9 %psum.14 = bf16[1024]{0:T(1024)(128)(2,1)S(1)} all-reduce(bf16[1024]{0:T(1024)(128)(2,1)S(1)} %fusion.2), channel_id=1, replica_groups=mesh['point'=16,'cent'=8] {'point'}, use_global_device_ids=true, to_apply=%region_1.0 | all-reduce | flops 1024 | bytes 4096 | tf_op jit(solution)/shard_map/psum | solution.py:27
  118.3 0.0 copy-start
  118.3 5.3 %multiply_reduce_fusion = f32[4096]{0:T(1024)S(1)} fusion(bf16[4096,1024]{1,0:T(8,128)(2,1)} %all-gather.3.cloned.1.call-done), kind=kLoop, calls=%fused_computation.4 | loop fusion | flops 12578816 | bytes 8404992 | tf_op jit(solution)/shard_map/reduce_sum | solution.py:34
  123.6 42.7 %all-reduce.2.cloned.1.call-done = bf16[1024,1024]{1,0:T(8,128)(2,1)} async-done(((bf16[1024,1024]{1,0:T(8,128)(2,1)}), bf16[1024,1024]{1,0:T(8,128)(2,1)}) %all-reduce.2.cloned.1.call-update) | async-done | bytes 2097168 | tf_op jit(solution)/shard_map/psum | solution.py:26
  166.3 0.0 copy-done
  166.3 0.0 copy-start.1
  166.3 3.0 %multiply_reduce_fusion.2 = f32[1024]{0:T(1024)S(1)} fusion(bf16[1024,1024]{1,0:T(8,128)(2,1)S(1)} %copy-done, f32[1024]{0:T(1024)S(1)} %convert_maximum_fusion, bf16[1024,1024]{1,0:T(8,128)(2,1)} %all-reduce.2.cloned.1.call-done, pred[1024]{0:T(1024)(128)(4,1)S(1)} %convert_compare_fusion), kind=kLoop, calls=%fused_computation.13 | loop fusion | flops 8387584 | bytes 4203520 | tf_op jit(solution)/shard_map/reduce_sum | solution.py:11
  169.3 0.0 copy-done.1
  169.3 2.0 multiply_reduce_fusion.1
  171.3 0.0 copy-start.2
  171.3 1.3 copy-done.2
  172.6 14.5 %bitcast_subtract_fusion = f32[4096,1024]{0,1:T(8,128)} fusion(bf16[1024,1024]{1,0:T(8,128)(2,1)S(1)} %get-tuple-element.9, bf16[4096,1024]{1,0:T(8,128)(2,1)} %all-gather.3.cloned.1.call-done, f32[1024]{0:T(1024)S(1)} %get-tuple-element.8, f32[4096]{0:T(1024)S(1)} %multiply_reduce_fusion), kind=kOutput, calls=%fused_computation.3 | convolution fusion | flops 8602517504 | bytes 27283456 | tf_op jit(solution)/shard_map/dot_general | solution.py:31
  187.1 17.4 %copy.7 = f32[4096,1024]{1,0:T(8,128)} copy(f32[4096,1024]{0,1:T(8,128)} %bitcast_subtract_fusion) | data formatting | bytes 33554432
  (4 shorter events, 0.0 us)
Async XLA Ops:
  7.2 54.8 %all-gather.3.cloned.1.call-start = ((), (), s32[]{:S(2)}) async-start(), calls=%async_computation | async-start | bytes 9437184 | tf_op jit(solution)/shard_map/all_gather | solution.py:18
  7.9 158.4 %all-reduce.2.cloned.1.call-start = ((), (), s32[]{:S(2)}) async-start(), calls=%async_computation.1 | async-start | bytes 4194304 | tf_op jit(solution)/shard_map/psum | solution.py:26
  118.3 48.0 %copy-start = (bf16[1024,1024]{1,0:T(8,128)(2,1)S(1)}, bf16[1024,1024]{1,0:T(8,128)(2,1)}, u32[]{:S(2)}) copy-start(bf16[1024,1024]{1,0:T(8,128)(2,1)} %param.5) | copy-start | bytes 6291460
  166.3 3.0 %copy-start.1 = (bf16[1024,1024]{1,0:T(8,128)(2,1)S(1)}, bf16[1024,1024]{1,0:T(8,128)(2,1)}, u32[]{:S(2)}) copy-start(bf16[1024,1024]{1,0:T(8,128)(2,1)} %all-reduce.2.cloned.1.call-done) | copy-start | bytes 6291460
  171.3 1.3 copy-start.2
Sparse Core Ops, SparseCore 0:
  9.7 52.1 all-gather.2
  75.6 90.6 all-reduce.1
where the time goes:
time: 212 us; the launch traced here: 211 us
  waiting for transfers between devices  85.1 us (40%)
  blocking collectives  53.2 us (25%)
  matrix products  28 us (13%)
  local copies, waits for them, and re-layouts  18.8 us (9%)
  between operations  14.1 us (7%)
  other arithmetic  12.2 us (6%)
    psum x1, waiting for transfers between devices, shards(): lax.psum(partial_rows.astype(jnp.bfloat16), 'point').astype(jnp.float32)  42.7 us
    all_gather x1, waiting for transfers between devices, shards(): lax.all_gather(points, 'cent', axis=0, tiled=True)  41.7 us
    psum x1, blocking collectives, shards(): lax.psum(partial_counts.astype(jnp.bfloat16), 'point').astype(jnp.float32)  40.9 us
    unnamed x7, local copies, waits for them, and re-layouts  18.8 us
    dot_general x1, matrix products, shards(): lax.dot_general(group_points, new_centroids, (((1,), (1,)), ((), ())), pr...  14.5 us
    dot_general x1, matrix products, shards(): jnp.dot(onehot, group_points, preferred_element_type=jnp.float32)  13.5 us
    all_gather x1, blocking collectives, shards(): lax.all_gather(assign, 'cent', axis=0, tiled=True)  12.3 us
    reduce_sum x1, other arithmetic, shards(): point_sq = jnp.sum(jnp.square(group_points.astype(jnp.float32)), axis=1)  5.28 us
  transfers between devices with their start and end apart: 2, of which 2 were waited for; matrix products, arithmetic and copies ran while one was open for 3% of the time, Pallas kernels for 0%

commit v1 on v0

v1 whole, which is shorter than its diff:
```python
import functools

import jax
import jax.numpy as jnp
from jax import lax
from jax.experimental import pallas as pl
from jax.experimental.pallas import tpu as pltpu
from jax.sharding import PartitionSpec as P

MESH = pl.DeviceIdType.MESH
F32, BF16 = jnp.float32, jnp.bfloat16
LANES = 128
GROUPS = (2, 2, 2, 1, 1)
DIGITS = 128


class Wires:
    def __init__(self, send, recv, local):
        self.send, self.recv, self.local = send, recv, local
        self.n_remote = self.n_local = 0
        self.sent, self.stored = [], []

    def remote(self, src, dst, target):
        index = self.n_remote
        self.n_remote += 1
        copy = pltpu.make_async_remote_copy(
            src_ref=src, dst_ref=dst, send_sem=self.send.at[index], recv_sem=self.recv.at[index],
            device_id=target, device_id_type=MESH,
        )
        copy.start()
        self.sent.append(copy)
        return copy

    def here(self, src, dst):
        copy = pltpu.make_async_copy(src, dst, self.local.at[self.n_local])
        self.n_local += 1
        copy.start()
        return copy


def gather_chunk(wires, buf, slot, up, down, sibling):
    rows = buf(0).shape[0]
    half = rows // 2

    def piece(k, part):
        return buf(k).at[pl.ds(part * half, half)]

    from_below = wires.remote(buf(0), buf(1), up)
    from_above = wires.remote(buf(0), buf(2), down)
    shared = [wires.remote(buf(0), buf(4), sibling)]
    yield
    from_below.wait_recv()
    far_a = wires.remote(piece(1, 0), piece(3, 0), up)
    shared.append(wires.remote(buf(1), buf(5), sibling))
    from_above.wait_recv()
    far_b = wires.remote(piece(2, 1), piece(3, 1), down)
    shared.append(wires.remote(buf(2), buf(6), sibling))
    yield
    far_a.wait_recv()
    shared.append(wires.remote(piece(3, 0), piece(7, 0), sibling))
    far_b.wait_recv()
    shared.append(wires.remote(piece(3, 1), piece(7, 1), sibling))
    yield
    for copy in shared:
        copy.wait_recv()
    yield


def gather_labels(wires, lab, up, down, sibling):
    from_below = wires.remote(lab.at[0], lab.at[1], up)
    from_above = wires.remote(lab.at[0], lab.at[2], down)
    shared = [wires.remote(lab.at[0], lab.at[4], sibling)]
    yield
    from_below.wait_recv()
    far = wires.remote(lab.at[1], lab.at[3], up)
    shared.append(wires.remote(lab.at[1], lab.at[5], sibling))
    from_above.wait_recv()
    shared.append(wires.remote(lab.at[2], lab.at[6], sibling))
    yield
    far.wait_recv()
    shared.append(wires.remote(lab.at[3], lab.at[7], sibling))
    yield
    for copy in shared:
        copy.wait_recv()
    yield


def add(*terms):
    total = terms[0].astype(F32)
    for term in terms[1:]:
        total = total + term.astype(F32)
    return total


def reduce_half(wires, base, first, second, first_ids, second_ids, part, land, cent, finish):
    a_up, a_down = first_ids
    b_up, b_down = second_ids

    def outer(k, start=0, size=128):
        return pl.ds(pl.multiple_of(base + lax.rem(first + 4 + k, 4) * 128 + start, 16), size)

    def inner(k, start=0, size=32):
        return pl.ds(pl.multiple_of(base + first * 128 + lax.rem(second + 4 + k, 4) * 32 + start, 16), size)

    def landing(start, size):
        return land.at[pl.ds(start, size)]

    one_a = wires.remote(part.at[outer(2, 0, 64)], landing(0, 64), a_up)
    one_b = wires.remote(part.at[outer(2, 64, 64)], landing(64, 64), a_down)
    yield
    one_a.wait_recv()
    part[outer(1, 0, 64)] = add(part[outer(1, 0, 64)], land[0:64]).astype(BF16)
    two_a = wires.remote(part.at[outer(1)], landing(128, 128), a_up)
    one_b.wait_recv()
    part[outer(-1, 64, 64)] = add(part[outer(-1, 64, 64)], land[64:128]).astype(BF16)
    two_b = wires.remote(part.at[outer(-1)], landing(256, 128), a_down)
    yield
    two_a.wait_recv()
    two_b.wait_recv()
    part[outer(0)] = add(part[outer(0)], land[128:256], land[256:384]).astype(BF16)
    three_a = wires.remote(part.at[inner(2, 0, 16)], landing(384, 16), b_up)
    three_b = wires.remote(part.at[inner(2, 16, 16)], landing(400, 16), b_down)
    yield
    three_a.wait_recv()
    part[inner(1, 0, 16)] = add(part[inner(1, 0, 16)], land[384:400]).astype(BF16)
    four_a = wires.remote(part.at[inner(1)], landing(416, 32), b_up)
    three_b.wait_recv()
    part[inner(-1, 16, 16)] = add(part[inner(-1, 16, 16)], land[400:416]).astype(BF16)
    four_b = wires.remote(part.at[inner(-1)], landing(448, 32), b_down)
    yield
    four_a.wait_recv()
    four_b.wait_recv()
    cent[inner(0)] = finish(add(part[inner(0)], land[416:448], land[448:480]))
    five_a = wires.remote(cent.at[inner(0)], cent.at[inner(0)], b_up)
    five_b = wires.remote(cent.at[inner(0)], cent.at[inner(0)], b_down)
    yield
    five_a.wait_recv()
    six_a = wires.remote(cent.at[inner(-1, 0, 16)], cent.at[inner(-1, 0, 16)], b_up)
    five_b.wait_recv()
    six_b = wires.remote(cent.at[inner(1, 16, 16)], cent.at[inner(1, 16, 16)], b_down)
    yield
    six_a.wait_recv()
    six_b.wait_recv()
    seven_a = wires.remote(cent.at[outer(0)], cent.at[outer(0)], a_up)
    seven_b = wires.remote(cent.at[outer(0)], cent.at[outer(0)], a_down)
    yield
    seven_a.wait_recv()
    eight_a = wires.remote(cent.at[outer(-1, 0, 64)], cent.at[outer(-1, 0, 64)], a_up)
    seven_b.wait_recv()
    eight_b = wires.remote(cent.at[outer(1, 64, 64)], cent.at[outer(1, 64, 64)], a_down)
    yield
    eight_a.wait_recv()
    eight_b.wait_recv()
    yield


def centroid_kernel(points, labels, old, all_points, blended, pts, lab, onehot, old_rows, weights, *rest):
    n_groups = len(GROUPS)
    parts, lands, cents = rest[:n_groups], rest[n_groups : 2 * n_groups], rest[2 * n_groups : 3 * n_groups]
    send, recv, local = rest[3 * n_groups :]
    wires = Wires(send, recv, local)
    p, c = lax.axis_index("point"), lax.axis_index("cent")
    x, z, y, core = p // 4, lax.rem(p, 4), c // 2, lax.rem(c, 2)

    def ring(k, by):
        return lax.rem(k + 4 + by, 4)

    up, down = ({"cent": ring(y, by) * 2 + core} for by in (1, -1))
    sibling = {"cent": y * 2 + 1 - core}
    x_ids = tuple({"point": ring(x, by) * 4 + z} for by in (1, -1))
    z_ids = tuple({"point": x * 4 + ring(z, by)} for by in (1, -1))

    rows = points.shape[0]
    loads = [wires.here(labels, lab.at[0]), wires.here(points, pts.at[pl.ds(0, rows)])]
    row_a = pl.multiple_of(x * 128 + z * 32, 32)
    row_b = pl.multiple_of(512 + z * 128 + x * 32, 32)
    old_loads = [wires.here(old.at[pl.ds(row_a, 32)], old_rows.at[0]), wires.here(old.at[pl.ds(row_b, 32)], old_rows.at[1])]

    barrier = pltpu.get_barrier_semaphore()
    for other in (up, down, sibling, *x_ids, *z_ids):
        pl.semaphore_signal(barrier, inc=1, device_id=other, device_id_type=MESH)
    pl.semaphore_wait(barrier, 7)
    for load in loads:
        load.wait()

    n_chunks = pts.shape[1] // LANES
    gathers = []

    def start_gather(t):
        if t < n_chunks:
            buf = lambda k: pts.at[pl.ds(k * rows, rows), pl.ds(t * LANES, LANES)]
            gathers.append(gather_chunk(wires, buf, None, up, down, sibling))
            next(gathers[t])

    label_gather = gather_labels(wires, lab, up, down, sibling)
    next(label_gather)
    start_gather(0)
    start_gather(1)
    for _ in range(3):
        next(label_gather)

    n_rows = onehot.shape[0]
    first_id = c * n_rows
    tile = 64

    @pl.loop(0, n_rows // tile)
    def _(r):
        row = pl.multiple_of(r * tile, tile)
        ids = first_id + row + lax.broadcasted_iota(jnp.int32, (tile, rows), 0)
        for k in range(8):
            same = ids == lab[k, 0:1, :]
            onehot[pl.ds(row, tile), k * rows : (k + 1) * rows] = jnp.where(same, 1.0, 0.0).astype(BF16)

    width0 = GROUPS[0] * LANES
    ones = jnp.ones((onehot.shape[1], DIGITS), BF16)

    @pl.loop(0, n_rows // 256)
    def _(r):
        row = pl.ds(pl.multiple_of(r * 256, 256), 256)
        count = jnp.dot(onehot[row, :], ones, preferred_element_type=F32).astype(jnp.int32)
        place = lax.broadcasted_iota(jnp.int32, count.shape, 1) & 3
        digit = lax.shift_right_logical(count, place * 4) & 15
        parts[0][row, width0:] = digit.astype(F32).astype(BF16)

    for load in old_loads:
        load.wait()

    def finisher(g, half):
        start = sum(GROUPS[:g]) * LANES
        width = GROUPS[g] * LANES

        def finish(total):
            if g == 0:
                place = lax.broadcasted_iota(jnp.int32, (32, DIGITS), 1)
                scale = jnp.where(place == 0, 1.0, jnp.where(place == 1, 16.0, jnp.where(place == 2, 256.0, 4096.0)))
                digits = jnp.where(place < 4, total[:, width:] * scale, 0.0)
                count = jnp.sum(digits, axis=1, keepdims=True)
                weights[half, 0] = jnp.broadcast_to(jnp.where(count > 0.0, 0.5 / jnp.maximum(count, 1.0), 0.0), (32, 128))
                weights[half, 1] = jnp.broadcast_to(jnp.where(count > 0.0, 0.5, 1.0), (32, 128))
            new_w, old_w = weights[half, 0][:, 0:1], weights[half, 1][:, 0:1]
            old_part = old_rows[half, :, start : start + width].astype(F32)
            return (total[:, :width] * new_w + old_part * old_w).astype(BF16)

        return finish

    flying = []

    def start_group(g):
        start, width = sum(GROUPS[:g]) * LANES, GROUPS[g] * LANES
        part = parts[g]

        @pl.loop(0, n_rows // 256)
        def _(r):
            row = pl.ds(pl.multiple_of(r * 256, 256), 256)
            sums = jnp.dot(onehot[row, :], pts[:, start : start + width], preferred_element_type=F32)
            part[row, 0:width] = sums.astype(BF16)

        halves = (
            reduce_half(wires, 0, x, z, x_ids, z_ids, part, lands[g].at[0], cents[g], finisher(g, 0)),
            reduce_half(wires, 512, z, x, z_ids, x_ids, part, lands[g].at[1], cents[g], finisher(g, 1)),
        )
        for half in halves:
            next(half)
        flying.append((g, halves))

    stores = []

    def advance():
        for entry in list(flying):
            g, halves = entry
            for half in halves:
                next(half)
            entry_steps[g] = entry_steps.get(g, 0) + 1
            if entry_steps[g] == 8:
                flying.remove(entry)
                start, width = sum(GROUPS[:g]) * LANES, GROUPS[g] * LANES
                stores.append(wires.here(cents[g], blended.at[:, pl.ds(start, width)]))

    entry_steps = {}
    ends = [sum(GROUPS[: g + 1]) for g in range(n_groups)]
    for t in range(n_chunks + 1):
        if t < n_chunks:
            next(gathers[t])
            start_gather(t + 2)
        advance()
        if t >= 1:
            next(gathers[t - 1])
            advance()
            next(gathers[t - 1])
            stores.append(wires.here(pts.at[:, pl.ds((t - 1) * LANES, LANES)], all_points.at[:, pl.ds((t - 1) * LANES, LANES)]))
            if t in ends:
                start_group(ends.index(t))
    while flying:
        advance()
    for copy in wires.sent:
        copy.wait_send()
    for copy in stores:
        copy.wait()


def distance_kernel(points, blended, new, out, cent_sq):
    @pl.when(pl.program_id(0) == 0)
    def _():
        ones = jnp.ones((8, blended.shape[1]), BF16)
        tile = 128

        for r in range(blended.shape[0] // tile):
            row = pl.ds(r * tile, tile)
            wide = blended[row, :].astype(F32)
            scale = lax.rsqrt(jnp.sum(wide * wide, axis=1, keepdims=True) + 1e-06)
            rounded = (wide * scale).astype(BF16)
            new[row, :] = rounded
            square = jnp.square(rounded.astype(F32))
            high = square.astype(BF16)
            low = (square - high.astype(F32)).astype(BF16)
            nt = (((1,), (1,)), ((), ()))
            cent_sq[:, r * tile : (r + 1) * tile] = lax.dot_general(
                ones, high, nt, preferred_element_type=F32
            ) + lax.dot_general(ones, low, nt, preferred_element_type=F32)

    block = points[...]
    wide = block.astype(F32)
    point_sq = jnp.sum(wide * wide, axis=1, keepdims=True)
    products = lax.dot_general(block, new[...], (((1,), (1,)), ((), ())), preferred_element_type=F32)
    out[...] = (point_sq + cent_sq[0:1, :]) - 2.0 * products


def block_of(k):
    c = lax.axis_index("cent")
    y, core = c // 2, lax.rem(c, 2)
    far, other = lax.rem(k, 4), k // 4
    shift = jnp.where(far == 0, 0, jnp.where(far == 1, 3, jnp.where(far == 2, 1, 2)))
    side = jnp.where(other == 0, core, 1 - core)
    return lax.rem(y + shift, 4) * 2 + side


def shards(points, assign, old_centroids):
    rows, width = points.shape
    n_rows = old_centroids.shape[0]
    labels = jnp.broadcast_to(assign[None, :], (8, rows))
    group = 8 * rows
    widths = [n * LANES for n in GROUPS]
    sums = [w + (DIGITS if g == 0 else 0) for g, w in enumerate(widths)]
    n_remote = 9 * (width // LANES) + 8 + 32 * len(GROUPS)
    everywhere = pl.BlockSpec(memory_space=pl.ANY)
    all_points, blended = pl.pallas_call(
        centroid_kernel,
        out_shape=(jax.ShapeDtypeStruct((group, width), BF16), jax.ShapeDtypeStruct((n_rows, width), BF16)),
        in_specs=[everywhere] * 3,
        out_specs=(everywhere, everywhere),
        scratch_shapes=[
            pltpu.VMEM((group, width), BF16),
            pltpu.VMEM((8, 8, rows), jnp.int32),
            pltpu.VMEM((n_rows, group), BF16),
            pltpu.VMEM((2, 32, width), BF16),
            pltpu.VMEM((2, 2, 32, 128), F32),
            *[pltpu.VMEM((n_rows, w), BF16) for w in sums],
            *[pltpu.VMEM((2, 480, w), BF16) for w in sums],
            *[pltpu.VMEM((n_rows, w), BF16) for w in widths],
            pltpu.SemaphoreType.DMA((n_remote,)),
            pltpu.SemaphoreType.DMA((n_remote,)),
            pltpu.SemaphoreType.DMA((4 + width // LANES + len(GROUPS),)),
        ],
        compiler_params=pltpu.CompilerParams(
            collective_id=0, has_side_effects=True, vmem_limit_bytes=40 * 2**20
        ),
        cost_estimate=pl.CostEstimate(flops=2 * n_rows * group * width, bytes_accessed=2 * group * width, transcendentals=0),
    )(points, labels, old_centroids)
    new_centroids, distances = pl.pallas_call(
        distance_kernel,
        grid=(8,),
        out_shape=(jax.ShapeDtypeStruct((n_rows, width), BF16), jax.ShapeDtypeStruct((group, n_rows), F32)),
        in_specs=[
            pl.BlockSpec((rows, width), lambda k: (k, 0)),
            pl.BlockSpec((n_rows, width), lambda k: (0, 0)),
        ],
        out_specs=(
            pl.BlockSpec((n_rows, width), lambda k: (0, 0)),
            pl.BlockSpec((rows, n_rows), lambda k: (block_of(k), 0)),
        ),
        scratch_shapes=[pltpu.VMEM((8, n_rows), F32)],
        compiler_params=pltpu.CompilerParams(vmem_limit_bytes=40 * 2**20),
        cost_estimate=pl.CostEstimate(
            flops=2 * n_rows * group * width, bytes_accessed=4 * group * n_rows + 2 * group * width, transcendentals=0
        ),
    )(all_points, blended)
    return new_centroids, distances


def solution(mesh):
    return jax.shard_map(
        shards,
        mesh=mesh,
        in_specs=(P(("point", "cent"), None), P(("point", "cent")), P("cent", None)),
        out_specs=(P("cent", None), P("point", "cent")),
        check_vma=False,
    )
```

time: 212 us -> 139 us (0.66)
  Pallas kernels: 0 us -> 135 us
  waiting for transfers between devices: 85.1 us -> 0 us
  blocking collectives: 53.2 us -> 0 us
  matrix products: 28 us -> 0 us
  local copies, waits for them, and re-layouts: 18.8 us -> 3.5 us
  between operations: 14.1 us -> 0.64 us
  other arithmetic: 12.2 us -> 0 us
    pallas_call x0 -> x2, Pallas kernels: none -> 135 us  [the longest x1 121 us: shards(): pl.pallas_call(centroid_kernel, out_shape=(jax.ShapeDtypeStruct((group, w...]
    psum x1 -> x0, waiting for transfers between devices: 42.7 us -> none  [shards(): lax.psum(partial_rows.astype(jnp.bfloat16), 'point').astype(jnp.float32)]
    all_gather x1 -> x0, waiting for transfers between devices: 41.7 us -> none  [shards(): lax.all_gather(points, 'cent', axis=0, tiled=True)]
    psum x1 -> x0, blocking collectives: 40.9 us -> none  [shards(): lax.psum(partial_counts.astype(jnp.bfloat16), 'point').astype(jnp.float32)]
    dot_general x2 -> x0, matrix products: 28 us -> none  [the longest x1 14.5 us: shards(): lax.dot_general(group_points, new_centroids, (((1,), (1,)), ((), ())), pr...]
    unnamed x7 -> x4, local copies, waits for them, and re-layouts: 18.8 us -> 2.81 us
    all_gather x1 -> x0, blocking collectives: 12.3 us -> none  [shards(): lax.all_gather(assign, 'cent', axis=0, tiled=True)]
    reduce_sum x4 -> x0, other arithmetic: 12.1 us -> none  [the longest x1 5.28 us: shards(): point_sq = jnp.sum(jnp.square(group_points.astype(jnp.float32)), axis=1)]
  transfers between devices with their start and end apart: 2 -> 0, of which waited for: 2 -> 0; matrix products, arithmetic and copies ran while one was open for 3% -> 0% of each run, Pallas kernels for 0% -> 0%
where the time goes in v1:
time: 139 us
  Pallas kernels  135 us (97%)
  local copies, waits for them, and re-layouts  3.5 us (3%)
    pallas_call x1, Pallas kernels, shards(): pl.pallas_call(centroid_kernel, out_shape=(jax.ShapeDtypeStruct((group, w...  121 us
    pallas_call x1, Pallas kernels, shards(): pl.pallas_call(distance_kernel, grid=(8,), out_shape=(jax.ShapeDtypeStruc...  14.1 us
    unnamed x4, local copies, waits for them, and re-layouts  2.81 us

profile of v1, /device:TPU:0, one launch (start us, length us, event | category | flops | bytes accessed | tf_op | source)
XLA Modules:
  0.0 139.0 jit_solution(14350630143377207556)
XLA Ops:
  0.6 0.7 broadcast_in_dim.2.labels
  1.3 0.0 copy-start
  1.3 1.6 %copy-done = bf16[1024,1024]{1,0:T(8,128)(2,1)S(1)} copy-done((bf16[1024,1024]{1,0:T(8,128)(2,1)S(1)}, bf16[1024,1024]{1,0:T(8,128)(2,1)}, u32[]{:S(2)}) %copy-start) | copy-done | bytes 2097176
  2.9 0.0 copy-start.1
  2.9 1.2 copy-done.1
  4.1 120.8 %shard_map.50 = (bf16[4096,1024]{1,0:T(8,128)(2,1)S(1)}, bf16[1024,1024]{1,0:T(8,128)(2,1)S(1)}) custom-call(bf16[512,1024]{1,0:T(8,128)(2,1)S(1)} %copy-done.1, s32[8,512]{1,0:T(8,128)S(1)} %broadcast_in_dim.2.labels, bf16[1024,1024]{1,0:T(8,128)(2,1)S(1)} %copy-done), custom_call_target="tpu_custom_call" | custom-call | flops 8589934592 | bytes 8388608 | tf_op jit(solution)/shard_map/pallas_call | solution.py:346
  125.0 14.1 %shard_map.51 = (bf16[1024,1024]{1,0:T(8,128)(2,1)}, f32[4096,1024]{1,0:T(8,128)}) custom-call(bf16[4096,1024]{1,0:T(8,128)(2,1)S(1)} %get-tuple-element.4.points, bf16[1024,1024]{1,0:T(8,128)(2,1)S(1)} %get-tuple-element.5.blended), custom_call_target="tpu_custom_call" | custom-call | flops 8589934592 | bytes 25165824 | tf_op jit(solution)/shard_map/pallas_call | solution.py:369
Async XLA Ops:
  1.3 1.6 %copy-start = (bf16[1024,1024]{1,0:T(8,128)(2,1)S(1)}, bf16[1024,1024]{1,0:T(8,128)(2,1)}, u32[]{:S(2)}) copy-start(bf16[1024,1024]{1,0:T(8,128)(2,1)} %old.1) | copy-start | bytes 6291460
  2.9 1.2 copy-start.1

commit v2 on v1

v2 whole, which is shorter than its diff:
```python
import functools

import jax
import jax.numpy as jnp
from jax import lax
from jax.experimental import pallas as pl
from jax.experimental.pallas import tpu as pltpu
from jax.sharding import PartitionSpec as P

MESH = pl.DeviceIdType.MESH
F32, BF16 = jnp.float32, jnp.bfloat16
LANES = 128
GROUPS = (2, 2, 2, 1, 1)
DIGITS = 128


class Wires:
    def __init__(self, send, recv, local):
        self.send, self.recv, self.local = send, recv, local
        self.n_remote = self.n_local = 0
        self.sent, self.stored = [], []

    def remote(self, src, dst, target):
        index = self.n_remote
        self.n_remote += 1
        copy = pltpu.make_async_remote_copy(
            src_ref=src, dst_ref=dst, send_sem=self.send.at[index], recv_sem=self.recv.at[index],
            device_id=target, device_id_type=MESH,
        )
        copy.start()
        self.sent.append(copy)
        return copy

    def here(self, src, dst):
        copy = pltpu.make_async_copy(src, dst, self.local.at[self.n_local])
        self.n_local += 1
        copy.start()
        return copy


def gather_chunk(wires, buf, up, down, sibling):
    half = buf(0).shape[0] // 2

    def piece(k, part):
        return buf(k).at[pl.ds(part * half, half)]

    from_below = wires.remote(buf(0), buf(1), up)
    from_above = wires.remote(buf(0), buf(2), down)
    near = [wires.remote(buf(0), buf(3), sibling)]
    yield
    from_below.wait_recv()
    far_a = wires.remote(piece(1, 0), piece(6, 0), up)
    from_above.wait_recv()
    far_b = wires.remote(piece(2, 1), piece(6, 1), down)
    near.append(wires.remote(buf(1), buf(4), sibling))
    near.append(wires.remote(buf(2), buf(5), sibling))
    yield
    for copy in near:
        copy.wait_recv()
    yield
    far_a.wait_recv()
    far = [wires.remote(piece(6, 0), piece(7, 0), sibling)]
    far_b.wait_recv()
    far.append(wires.remote(piece(6, 1), piece(7, 1), sibling))
    yield
    for copy in far:
        copy.wait_recv()
    yield


def gather_labels(wires, lab, up, down, across, sibling):
    first = [wires.remote(lab.at[0], lab.at[k], target) for k, target in ((6, across), (1, up), (2, down))]
    near = [wires.remote(lab.at[0], lab.at[3], sibling)]
    yield
    for copy, k, to in zip(first[1:] + first[:1], (1, 2, 6), (4, 5, 7)):
        copy.wait_recv()
        near.append(wires.remote(lab.at[k], lab.at[to], sibling))
    yield
    for copy in near:
        copy.wait_recv()
    yield


def add(*terms):
    total = terms[0].astype(F32)
    for term in terms[1:]:
        total = total + term.astype(F32)
    return total


def reduce_half(wires, base, first, second, first_ids, second_ids, part, land, cent, finish):
    order = (2, 1, 3)

    def outer(k):
        return pl.ds(pl.multiple_of(base + lax.rem(first + k, 4) * 128, 128), 128)

    def inner(k):
        return pl.ds(pl.multiple_of(base + first * 128 + lax.rem(second + k, 4) * 32, 32), 32)

    copies = [wires.remote(part.at[outer(k)], land.at[pl.ds((k - 1) * 128, 128)], first_ids[k]) for k in order]
    yield
    for copy in copies:
        copy.wait_recv()
    part[outer(0)] = add(part[outer(0)], land[0:128], land[128:256], land[256:384]).astype(BF16)
    copies = [wires.remote(part.at[inner(k)], land.at[pl.ds(352 + k * 32, 32)], second_ids[k]) for k in order]
    yield
    for copy in copies:
        copy.wait_recv()
    cent[inner(0)] = finish(add(part[inner(0)], land[384:416], land[416:448], land[448:480]))
    copies = [wires.remote(cent.at[inner(0)], cent.at[inner(0)], second_ids[k]) for k in order]
    yield
    for copy in copies:
        copy.wait_recv()
    copies = [wires.remote(cent.at[outer(0)], cent.at[outer(0)], first_ids[k]) for k in order]
    yield
    for copy in copies:
        copy.wait_recv()
    yield


def centroid_kernel(points, labels, old, all_points, blended, pts, lab, onehot, old_rows, weights, held, *rest):
    n_groups = len(GROUPS)
    parts, lands, cents = rest[:n_groups], rest[n_groups : 2 * n_groups], rest[2 * n_groups : 3 * n_groups]
    send, recv, local = rest[3 * n_groups :]
    wires = Wires(send, recv, local)
    p, c = lax.axis_index("point"), lax.axis_index("cent")
    x, z, y, core = p // 4, lax.rem(p, 4), c // 2, lax.rem(c, 2)

    def ring(k, by):
        return lax.rem(k + 4 + by, 4)

    up, across, down = ({"cent": ring(y, by) * 2 + core} for by in (1, 2, 3))
    sibling = {"cent": y * 2 + 1 - core}
    x_ids = {by: {"point": ring(x, by) * 4 + z} for by in (1, 2, 3)}
    z_ids = {by: {"point": x * 4 + ring(z, by)} for by in (1, 2, 3)}
    partners = (up, across, down, sibling, *x_ids.values(), *z_ids.values())

    rows = points.shape[0]
    loads = [wires.here(labels, lab.at[0]), wires.here(points, pts.at[pl.ds(0, rows)])]
    row_a = pl.multiple_of(x * 128 + z * 32, 32)
    row_b = pl.multiple_of(512 + z * 128 + x * 32, 32)
    old_loads = [wires.here(old.at[pl.ds(row_a, 32)], old_rows.at[0]), wires.here(old.at[pl.ds(row_b, 32)], old_rows.at[1])]

    barrier = pltpu.get_barrier_semaphore()
    for other in partners:
        pl.semaphore_signal(barrier, inc=1, device_id=other, device_id_type=MESH)
    pl.semaphore_wait(barrier, len(partners))
    for load in loads:
        load.wait()

    n_chunks = pts.shape[1] // LANES
    gathers = []

    def start_gather(t):
        if t < n_chunks:
            buf = lambda k: pts.at[pl.ds(k * rows, rows), pl.ds(t * LANES, LANES)]
            gathers.append(gather_chunk(wires, buf, up, down, sibling))
            next(gathers[t])

    label_gather = gather_labels(wires, lab, up, down, across, sibling)
    next(label_gather)
    start_gather(0)
    start_gather(1)

    n_rows = onehot.shape[0]
    first_id = c * n_rows
    tile = 64

    def match(slots):
        @pl.loop(0, n_rows // tile)
        def _(r):
            row = pl.multiple_of(r * tile, tile)
            ids = first_id + row + lax.broadcasted_iota(jnp.int32, (tile, rows), 0)
            for k in slots:
                same = ids == lab[k, 0:1, :]
                onehot[pl.ds(row, tile), k * rows : (k + 1) * rows] = jnp.where(same, 1.0, 0.0).astype(BF16)

    width0 = GROUPS[0] * LANES

    def count_digits():
        ones = jnp.ones((onehot.shape[1], DIGITS), BF16)

        @pl.loop(0, n_rows // 256)
        def _(r):
            row = pl.ds(pl.multiple_of(r * 256, 256), 256)
            count = jnp.dot(onehot[row, :], ones, preferred_element_type=F32).astype(jnp.int32)
            place = lax.broadcasted_iota(jnp.int32, count.shape, 1) & 3
            digit = lax.shift_right_logical(count, place * 4) & 15
            parts[0][row, width0:] = digit.astype(F32).astype(BF16)

    def finisher(g, half):
        start = sum(GROUPS[:g]) * LANES
        width = GROUPS[g] * LANES

        def finish(total):
            if g == 0:
                place = lax.broadcasted_iota(jnp.int32, (32, DIGITS), 1)
                scale = jnp.where(place == 0, 1.0, jnp.where(place == 1, 16.0, jnp.where(place == 2, 256.0, 4096.0)))
                digits = jnp.where(place < 4, total[:, width:] * scale, 0.0)
                count = jnp.sum(digits, axis=1, keepdims=True)
                weights[half, 0] = jnp.broadcast_to(jnp.where(count > 0.0, 0.5 / jnp.maximum(count, 1.0), 0.0), (32, 128))
                weights[half, 1] = jnp.broadcast_to(jnp.where(count > 0.0, 0.5, 1.0), (32, 128))
            new_w, old_w = weights[half, 0][:, 0:1], weights[half, 1][:, 0:1]
            old_part = old_rows[half, :, start : start + width].astype(F32)
            return (total[:, :width] * new_w + old_part * old_w).astype(BF16)

        return finish

    flying = []

    near_rows = 6 * rows

    def sum_near(g):
        start, width = sum(GROUPS[:g]) * LANES, GROUPS[g] * LANES

        @pl.loop(0, n_rows // 256)
        def _(r):
            row = pl.ds(pl.multiple_of(r * 256, 256), 256)
            held[row, 0:width] = jnp.dot(
                onehot[row, 0:near_rows], pts[0:near_rows, start : start + width], preferred_element_type=F32
            )

    def start_group(g, split):
        start, width = sum(GROUPS[:g]) * LANES, GROUPS[g] * LANES
        part = parts[g]

        @pl.loop(0, n_rows // 256)
        def _(r):
            row = pl.ds(pl.multiple_of(r * 256, 256), 256)
            if split:
                sums = held[row, 0:width] + jnp.dot(
                    onehot[row, near_rows:], pts[near_rows:, start : start + width], preferred_element_type=F32
                )
            else:
                sums = jnp.dot(onehot[row, :], pts[:, start : start + width], preferred_element_type=F32)
            part[row, 0:width] = sums.astype(BF16)

        halves = (
            reduce_half(wires, 0, x, z, x_ids, z_ids, part, lands[g].at[0], cents[g], finisher(g, 0)),
            reduce_half(wires, 512, z, x, z_ids, x_ids, part, lands[g].at[1], cents[g], finisher(g, 1)),
        )
        for half in halves:
            next(half)
        flying.append((g, halves))

    stores, steps = [], [0] * n_groups

    def advance():
        for entry in list(flying):
            g, halves = entry
            for half in halves:
                next(half)
            steps[g] += 1
            if steps[g] == 4:
                flying.remove(entry)
                start, width = sum(GROUPS[:g]) * LANES, GROUPS[g] * LANES
                stores.append(wires.here(cents[g], blended.at[:, pl.ds(start, width)]))

    def store_points(t):
        lanes = pl.ds(t * LANES, LANES)
        stores.append(wires.here(pts.at[:, lanes], all_points.at[:, lanes]))

    def complete(t):
        next(gathers[t])
        store_points(t)
        if t + 1 in ends:
            start_group(ends.index(t + 1), False)

    ends = [sum(GROUPS[: g + 1]) for g in range(n_groups)]
    next(label_gather)
    for t in range(n_chunks):
        next(gathers[t])
        start_gather(t + 2)
        advance()
        if t == 0:
            next(label_gather)
            match(range(4))
        if t == 1:
            match(range(4, 8))
        if t == 2:
            count_digits()
            for load in old_loads:
                load.wait()
        if t >= 1:
            next(gathers[t - 1])
            next(gathers[t - 1])
        if t >= 2:
            complete(t - 2)
    last = n_chunks - 1
    complete(last - 1)
    next(gathers[last])
    sum_near(n_groups - 1)
    next(gathers[last])
    next(gathers[last])
    start_group(n_groups - 1, True)
    store_points(last)
    while flying:
        advance()
    for copy in wires.sent:
        copy.wait_send()
    for copy in stores:
        copy.wait()


def distance_kernel(points, blended, new, out, cent_sq):
    @pl.when(pl.program_id(0) == 0)
    def _():
        ones = jnp.ones((8, blended.shape[1]), BF16)
        tile = 128

        for r in range(blended.shape[0] // tile):
            row = pl.ds(r * tile, tile)
            wide = blended[row, :].astype(F32)
            scale = lax.rsqrt(jnp.sum(wide * wide, axis=1, keepdims=True) + 1e-06)
            rounded = (wide * scale).astype(BF16)
            new[row, :] = rounded
            square = jnp.square(rounded.astype(F32))
            high = square.astype(BF16)
            low = (square - high.astype(F32)).astype(BF16)
            nt = (((1,), (1,)), ((), ()))
            cent_sq[:, r * tile : (r + 1) * tile] = lax.dot_general(
                ones, high, nt, preferred_element_type=F32
            ) + lax.dot_general(ones, low, nt, preferred_element_type=F32)

    block = points[...]
    wide = block.astype(F32)
    point_sq = jnp.sum(wide * wide, axis=1, keepdims=True)
    products = lax.dot_general(block, new[...], (((1,), (1,)), ((), ())), preferred_element_type=F32)
    out[...] = (point_sq + cent_sq[0:1, :]) - 2.0 * products


def block_of(k):
    c = lax.axis_index("cent")
    y, core = c // 2, lax.rem(c, 2)
    near = lax.rem(k, 3)
    shift = jnp.where(k >= 6, 2, jnp.where(near == 1, 3, jnp.where(near == 2, 1, 0)))
    sibling = (k == 7) | ((k >= 3) & (k < 6))
    return lax.rem(y + shift, 4) * 2 + jnp.where(sibling, 1 - core, core)


def shards(points, assign, old_centroids):
    rows, width = points.shape
    n_rows = old_centroids.shape[0]
    labels = jnp.broadcast_to(assign[None, :], (8, rows))
    group = 8 * rows
    widths = [n * LANES for n in GROUPS]
    sums = [w + (DIGITS if g == 0 else 0) for g, w in enumerate(widths)]
    n_remote = 9 * (width // LANES) + 7 + 24 * len(GROUPS)
    everywhere = pl.BlockSpec(memory_space=pl.ANY)
    all_points, blended = pl.pallas_call(
        centroid_kernel,
        out_shape=(jax.ShapeDtypeStruct((group, width), BF16), jax.ShapeDtypeStruct((n_rows, width), BF16)),
        in_specs=[everywhere] * 3,
        out_specs=(everywhere, everywhere),
        scratch_shapes=[
            pltpu.VMEM((group, width), BF16),
            pltpu.VMEM((8, 8, rows), jnp.int32),
            pltpu.VMEM((n_rows, group), BF16),
            pltpu.VMEM((2, 32, width), BF16),
            pltpu.VMEM((2, 2, 32, 128), F32),
            pltpu.VMEM((n_rows, GROUPS[-1] * LANES), F32),
            *[pltpu.VMEM((n_rows, w), BF16) for w in sums],
            *[pltpu.VMEM((2, 480, w), BF16) for w in sums],
            *[pltpu.VMEM((n_rows, w), BF16) for w in widths],
            pltpu.SemaphoreType.DMA((n_remote,)),
            pltpu.SemaphoreType.DMA((n_remote,)),
            pltpu.SemaphoreType.DMA((4 + width // LANES + len(GROUPS),)),
        ],
        compiler_params=pltpu.CompilerParams(
            collective_id=0, has_side_effects=True, vmem_limit_bytes=40 * 2**20
        ),
        cost_estimate=pl.CostEstimate(flops=2 * n_rows * group * width, bytes_accessed=2 * group * width, transcendentals=0),
    )(*(pltpu.with_memory_space_constraint(a, pltpu.HBM) for a in (points, labels, old_centroids)))
    new_centroids, distances = pl.pallas_call(
        distance_kernel,
        grid=(8,),
        out_shape=(jax.ShapeDtypeStruct((n_rows, width), BF16), jax.ShapeDtypeStruct((group, n_rows), F32)),
        in_specs=[
            pl.BlockSpec((rows, width), lambda k: (k, 0)),
            pl.BlockSpec((n_rows, width), lambda k: (0, 0)),
        ],
        out_specs=(
            pl.BlockSpec((n_rows, width), lambda k: (0, 0)),
            pl.BlockSpec((rows, n_rows), lambda k: (block_of(k), 0)),
        ),
        scratch_shapes=[pltpu.VMEM((8, n_rows), F32)],
        compiler_params=pltpu.CompilerParams(vmem_limit_bytes=40 * 2**20),
        cost_estimate=pl.CostEstimate(
            flops=2 * n_rows * group * width, bytes_accessed=4 * group * n_rows + 2 * group * width, transcendentals=0
        ),
    )(all_points, blended)
    return new_centroids, distances


def solution(mesh):
    return jax.shard_map(
        shards,
        mesh=mesh,
        in_specs=(P(("point", "cent"), None), P(("point", "cent")), P("cent", None)),
        out_specs=(P("cent", None), P("point", "cent")),
        check_vma=False,
    )
```

time: 139 us -> 101 us (0.73)
  Pallas kernels: 135 us -> 98.4 us
  local copies, waits for them, and re-layouts: 3.5 us -> 1.29 us
    pallas_call x1, Pallas kernels: 121 us -> 84.5 us  [shards(): pl.pallas_call(centroid_kernel, out_shape=(jax.ShapeDtypeStruct((group, w...]
    unnamed x4 -> x0, local copies, waits for them, and re-layouts: 2.81 us -> none
where the time goes in v2:
time: 101 us; the launch traced here: 100 us
  Pallas kernels  98.4 us (97%)
  local copies, waits for them, and re-layouts  1.29 us (1%)
    pallas_call x1, Pallas kernels, shards(): pl.pallas_call(centroid_kernel, out_shape=(jax.ShapeDtypeStruct((group, w...  84.5 us
    pallas_call x1, Pallas kernels, shards(): pl.pallas_call(distance_kernel, grid=(8,), out_shape=(jax.ShapeDtypeStruc...  13.9 us

profile of v2, /device:TPU:0, one launch (start us, length us, event | category | flops | bytes accessed | tf_op | source)
XLA Modules:
  0.0 100.3 jit_solution(11347387530643835303)
XLA Ops:
  0.6 1.3 %broadcast_in_dim.2.labels = s32[8,512]{1,0:T(8,128)} broadcast(s32[512]{0:T(512)} %param.4), dimensions={1} | broadcast | bytes 18432 | tf_op jit(solution)/shard_map/broadcast_in_dim | solution.py:344
  1.9 84.5 %shard_map.50 = (bf16[4096,1024]{1,0:T(8,128)(2,1)S(1)}, bf16[1024,1024]{1,0:T(8,128)(2,1)S(1)}) custom-call(bf16[512,1024]{1,0:T(8,128)(2,1)} %points.1, s32[8,512]{1,0:T(8,128)} %broadcast_in_dim.2.labels, bf16[1024,1024]{1,0:T(8,128)(2,1)} %old.1), custom_call_target="tpu_custom_call" | custom-call | flops 8589934592 | bytes 8388608 | tf_op jit(solution)/shard_map/pallas_call | solution.py:350
  86.4 13.9 %shard_map.51 = (bf16[1024,1024]{1,0:T(8,128)(2,1)}, f32[4096,1024]{1,0:T(8,128)}) custom-call(bf16[4096,1024]{1,0:T(8,128)(2,1)S(1)} %get-tuple-element.4.points, bf16[1024,1024]{1,0:T(8,128)(2,1)S(1)} %get-tuple-element.5.blended), custom_call_target="tpu_custom_call" | custom-call | flops 8589934592 | bytes 25165824 | tf_op jit(solution)/shard_map/pallas_call | solution.py:374

commit v3 on v2

--- a/solution.py
+++ b/solution.py
@@ -9,8 +9,7 @@
 
 MESH = pl.DeviceIdType.MESH
 F32, BF16 = jnp.float32, jnp.bfloat16
-LANES = 128
-GROUPS = (2, 2, 2, 1, 1)
+LANES = 256
 DIGITS = 128
 
 
@@ -38,33 +37,24 @@
         return copy
 
 
-def gather_chunk(wires, buf, up, down, sibling):
-    half = buf(0).shape[0] // 2
-
-    def piece(k, part):
-        return buf(k).at[pl.ds(part * half, half)]
-
-    from_below = wires.remote(buf(0), buf(1), up)
-    from_above = wires.remote(buf(0), buf(2), down)
-    near = [wires.remote(buf(0), buf(3), sibling)]
+def gather_chunk(wires, block, rows, up, down, sibling):
+    half = rows // 2
+    from_below = wires.remote(block(0, rows), block(rows, rows), up)
+    from_above = wires.remote(block(0, rows), block(2 * rows, rows), down)
     yield
     from_below.wait_recv()
-    far_a = wires.remote(piece(1, 0), piece(6, 0), up)
+    far_a = wires.remote(block(rows, half), block(6 * rows, half), up)
     from_above.wait_recv()
-    far_b = wires.remote(piece(2, 1), piece(6, 1), down)
-    near.append(wires.remote(buf(1), buf(4), sibling))
-    near.append(wires.remote(buf(2), buf(5), sibling))
-    yield
-    for copy in near:
-        copy.wait_recv()
+    far_b = wires.remote(block(2 * rows + half, half), block(6 * rows + half, half), down)
+    near = wires.remote(block(0, 3 * rows), block(3 * rows, 3 * rows), sibling)
+    yield
+    near.wait_recv()
     yield
     far_a.wait_recv()
-    far = [wires.remote(piece(6, 0), piece(7, 0), sibling)]
     far_b.wait_recv()
-    far.append(wires.remote(piece(6, 1), piece(7, 1), sibling))
-    yield
-    for copy in far:
-        copy.wait_recv()
+    far = wires.remote(block(6 * rows, rows), block(7 * rows, rows), sibling)
+    yield
+    far.wait_recv()
     yield
 
 
@@ -119,7 +109,7 @@
 
 
 def centroid_kernel(points, labels, old, all_points, blended, pts, lab, onehot, old_rows, weights, held, *rest):
-    n_groups = len(GROUPS)
+    n_groups = len(rest) // 3 - 1
     parts, lands, cents = rest[:n_groups], rest[n_groups : 2 * n_groups], rest[2 * n_groups : 3 * n_groups]
     send, recv, local = rest[3 * n_groups :]
     wires = Wires(send, recv, local)
@@ -153,8 +143,8 @@
 
     def start_gather(t):
         if t < n_chunks:
-            buf = lambda k: pts.at[pl.ds(k * rows, rows), pl.ds(t * LANES, LANES)]
-            gathers.append(gather_chunk(wires, buf, up, down, sibling))
+            block = lambda row, count: pts.at[pl.ds(row, count), pl.ds(t * LANES, LANES)]
+            gathers.append(gather_chunk(wires, block, rows, up, down, sibling))
             next(gathers[t])
 
     label_gather = gather_labels(wires, lab, up, down, across, sibling)
@@ -175,8 +165,6 @@
                 same = ids == lab[k, 0:1, :]
                 onehot[pl.ds(row, tile), k * rows : (k + 1) * rows] = jnp.where(same, 1.0, 0.0).astype(BF16)
 
-    width0 = GROUPS[0] * LANES
-
     def count_digits():
         ones = jnp.ones((onehot.shape[1], DIGITS), BF16)
 
@@ -186,11 +174,10 @@
             count = jnp.dot(onehot[row, :], ones, preferred_element_type=F32).astype(jnp.int32)
             place = lax.broadcasted_iota(jnp.int32, count.shape, 1) & 3
             digit = lax.shift_right_logical(count, place * 4) & 15
-            parts[0][row, width0:] = digit.astype(F32).astype(BF16)
+            parts[0][row, LANES:] = digit.astype(F32).astype(BF16)
 
     def finisher(g, half):
-        start = sum(GROUPS[:g]) * LANES
-        width = GROUPS[g] * LANES
+        start, width = g * LANES, LANES
 
         def finish(total):
             if g == 0:
@@ -206,96 +193,96 @@
 
         return finish
 
-    flying = []
-
     near_rows = 6 * rows
+    halves, stores = {}, []
 
     def sum_near(g):
-        start, width = sum(GROUPS[:g]) * LANES, GROUPS[g] * LANES
-
         @pl.loop(0, n_rows // 256)
         def _(r):
             row = pl.ds(pl.multiple_of(r * 256, 256), 256)
-            held[row, 0:width] = jnp.dot(
-                onehot[row, 0:near_rows], pts[0:near_rows, start : start + width], preferred_element_type=F32
+            held[row, :] = jnp.dot(
+                onehot[row, 0:near_rows], pts[0:near_rows, g * LANES : (g + 1) * LANES], preferred_element_type=F32
             )
 
-    def start_group(g, split):
-        start, width = sum(GROUPS[:g]) * LANES, GROUPS[g] * LANES
-        part = parts[g]
+    def reduce(g, split=False):
+        lanes = slice(g * LANES, (g + 1) * LANES)
 
         @pl.loop(0, n_rows // 256)
         def _(r):
             row = pl.ds(pl.multiple_of(r * 256, 256), 256)
             if split:
-                sums = held[row, 0:width] + jnp.dot(
-                    onehot[row, near_rows:], pts[near_rows:, start : start + width], preferred_element_type=F32
-                )
+                sums = held[row, :] + jnp.dot(onehot[row, near_rows:], pts[near_rows:, lanes], preferred_element_type=F32)
             else:
-                sums = jnp.dot(onehot[row, :], pts[:, start : start + width], preferred_element_type=F32)
-            part[row, 0:width] = sums.astype(BF16)
-
-        halves = (
-            reduce_half(wires, 0, x, z, x_ids, z_ids, part, lands[g].at[0], cents[g], finisher(g, 0)),
-            reduce_half(wires, 512, z, x, z_ids, x_ids, part, lands[g].at[1], cents[g], finisher(g, 1)),
+                sums = jnp.dot(onehot[row, :], pts[:, lanes], preferred_element_type=F32)
+            parts[g][row, 0:LANES] = sums.astype(BF16)
+
+        halves[g] = (
+            reduce_half(wires, 0, x, z, x_ids, z_ids, parts[g], lands[g].at[0], cents[g], finisher(g, 0)),
+            reduce_half(wires, 512, z, x, z_ids, x_ids, parts[g], lands[g].at[1], cents[g], finisher(g, 1)),
         )
-        for half in halves:
-            next(half)
-        flying.append((g, halves))
-
-    stores, steps = [], [0] * n_groups
-
-    def advance():
-        for entry in list(flying):
-            g, halves = entry
-            for half in halves:
+        advance(g)
+
+    def advance(*groups):
+        for g in groups:
+            for half in halves[g]:
                 next(half)
-            steps[g] += 1
-            if steps[g] == 4:
-                flying.remove(entry)
-                start, width = sum(GROUPS[:g]) * LANES, GROUPS[g] * LANES
-                stores.append(wires.here(cents[g], blended.at[:, pl.ds(start, width)]))
+
+    def gathered(t):
+        next(gathers[t])
 
     def store_points(t):
         lanes = pl.ds(t * LANES, LANES)
         stores.append(wires.here(pts.at[:, lanes], all_points.at[:, lanes]))
 
-    def complete(t):
-        next(gathers[t])
+    def store_centroids(g):
+        stores.append(wires.here(cents[g], blended.at[:, pl.ds(g * LANES, LANES)]))
+
+    next(label_gather)
+    next(label_gather)
+    match(range(4))
+    gathered(0)
+    start_gather(2)
+    match(range(4, 8))
+    count_digits()
+    for load in old_loads:
+        load.wait()
+    gathered(0)
+    gathered(1)
+    start_gather(3)
+    gathered(0)
+    gathered(0)
+    reduce(0)
+    gathered(1)
+    gathered(2)
+    gathered(1)
+    advance(0)
+    gathered(1)
+    reduce(1)
+    advance(0)
+    gathered(2)
+    gathered(2)
+    gathered(3)
+    advance(0)
+    gathered(2)
+    reduce(2)
+    for t in range(3):
         store_points(t)
-        if t + 1 in ends:
-            start_group(ends.index(t + 1), False)
-
-    ends = [sum(GROUPS[: g + 1]) for g in range(n_groups)]
-    next(label_gather)
-    for t in range(n_chunks):
-        next(gathers[t])
-        start_gather(t + 2)
-        advance()
-        if t == 0:
-            next(label_gather)
-            match(range(4))
-        if t == 1:
-            match(range(4, 8))
-        if t == 2:
-            count_digits()
-            for load in old_loads:
-                load.wait()
-        if t >= 1:
-            next(gathers[t - 1])
-            next(gathers[t - 1])
-        if t >= 2:
-            complete(t - 2)
-    last = n_chunks - 1
-    complete(last - 1)
-    next(gathers[last])
-    sum_near(n_groups - 1)
-    next(gathers[last])
-    next(gathers[last])
-    start_group(n_groups - 1, True)
-    store_points(last)
-    while flying:
-        advance()
+    advance(1)
+    gathered(3)
+    sum_near(3)
+    gathered(3)
+    advance(1)
+    gathered(3)
+    reduce(3, split=True)
+    store_points(3)
+    advance(0, 1, 2, 3)
+    store_centroids(0)
+    advance(1, 2, 3)
+    store_centroids(1)
+    advance(2, 3)
+    advance(2, 3)
+    store_centroids(2)
+    store_centroids(3)
     for copy in wires.sent:
         copy.wait_send()
     for copy in stores:
@@ -343,9 +330,9 @@
     n_rows = old_centroids.shape[0]
     labels = jnp.broadcast_to(assign[None, :], (8, rows))
     group = 8 * rows
-    widths = [n * LANES for n in GROUPS]
-    sums = [w + (DIGITS if g == 0 else 0) for g, w in enumerate(widths)]
-    n_remote = 9 * (width // LANES) + 7 + 24 * len(GROUPS)
+    n_chunks = width // LANES
+    sums = [LANES + (DIGITS if g == 0 else 0) for g in range(n_chunks)]
+    n_remote = (6 + 24) * n_chunks + 8
     everywhere = pl.BlockSpec(memory_space=pl.ANY)
     all_points, blended = pl.pallas_call(
         centroid_kernel,
@@ -358,13 +345,13 @@
             pltpu.VMEM((n_rows, group), BF16),
             pltpu.VMEM((2, 32, width), BF16),
             pltpu.VMEM((2, 2, 32, 128), F32),
-            pltpu.VMEM((n_rows, GROUPS[-1] * LANES), F32),
+            pltpu.VMEM((n_rows, LANES), F32),
             *[pltpu.VMEM((n_rows, w), BF16) for w in sums],
             *[pltpu.VMEM((2, 480, w), BF16) for w in sums],
-            *[pltpu.VMEM((n_rows, w), BF16) for w in widths],
+            *[pltpu.VMEM((n_rows, LANES), BF16) for _ in sums],
             pltpu.SemaphoreType.DMA((n_remote,)),
             pltpu.SemaphoreType.DMA((n_remote,)),
-            pltpu.SemaphoreType.DMA((4 + width // LANES + len(GROUPS),)),
+            pltpu.SemaphoreType.DMA((4 + 2 * n_chunks,)),
         ],
         compiler_params=pltpu.CompilerParams(
             collective_id=0, has_side_effects=True, vmem_limit_bytes=40 * 2**20

time: 101 us -> 91.8 us (0.909)
  Pallas kernels: 98.4 us -> 89.7 us
    pallas_call x1, Pallas kernels: 84.5 us -> 75.9 us  [shards(): pl.pallas_call(centroid_kernel, out_shape=(jax.ShapeDtypeStruct((group, w...]
where the time goes in v3:
time: 91.8 us; the launch traced here: 91.7 us
  Pallas kernels  89.7 us (98%)
  local copies, waits for them, and re-layouts  1.29 us (1%)
    pallas_call x1, Pallas kernels, shards(): pl.pallas_call(centroid_kernel, out_shape=(jax.ShapeDtypeStruct((group, w...  75.9 us
    pallas_call x1, Pallas kernels, shards(): pl.pallas_call(distance_kernel, grid=(8,), out_shape=(jax.ShapeDtypeStruc...  13.9 us

profile of v3, /device:TPU:0, one launch (start us, length us, event | category | flops | bytes accessed | tf_op | source)
XLA Modules:
  0.0 91.7 jit_solution(2401604197544507825)
XLA Ops:
  0.6 1.3 %broadcast_in_dim.2.labels = s32[8,512]{1,0:T(8,128)} broadcast(s32[512]{0:T(512)} %param.4), dimensions={1} | broadcast | bytes 18432 | tf_op jit(solution)/shard_map/broadcast_in_dim | solution.py:331
  1.9 75.9 %shard_map.50 = (bf16[4096,1024]{1,0:T(8,128)(2,1)S(1)}, bf16[1024,1024]{1,0:T(8,128)(2,1)S(1)}) custom-call(bf16[512,1024]{1,0:T(8,128)(2,1)} %points.1, s32[8,512]{1,0:T(8,128)} %broadcast_in_dim.2.labels, bf16[1024,1024]{1,0:T(8,128)(2,1)} %old.1), custom_call_target="tpu_custom_call" | custom-call | flops 8589934592 | bytes 8388608 | tf_op jit(solution)/shard_map/pallas_call | solution.py:337
  77.8 13.9 %shard_map.51 = (bf16[1024,1024]{1,0:T(8,128)(2,1)}, f32[4096,1024]{1,0:T(8,128)}) custom-call(bf16[4096,1024]{1,0:T(8,128)(2,1)S(1)} %get-tuple-element.4.points, bf16[1024,1024]{1,0:T(8,128)(2,1)S(1)} %get-tuple-element.5.blended), custom_call_target="tpu_custom_call" | custom-call | flops 8589934592 | bytes 25165824 | tf_op jit(solution)/shard_map/pallas_call | solution.py:361

commit v4 on v3

--- a/solution.py
+++ b/solution.py
@@ -9,7 +9,8 @@
 
 MESH = pl.DeviceIdType.MESH
 F32, BF16 = jnp.float32, jnp.bfloat16
-LANES = 256
+WIDTHS = (256, 256, 256, 128, 128)
+STARTS = tuple(sum(WIDTHS[:t]) for t in range(len(WIDTHS)))
 DIGITS = 128
 
 
@@ -108,10 +109,10 @@
     yield
 
 
-def centroid_kernel(points, labels, old, all_points, blended, pts, lab, onehot, old_rows, weights, held, *rest):
-    n_groups = len(rest) // 3 - 1
-    parts, lands, cents = rest[:n_groups], rest[n_groups : 2 * n_groups], rest[2 * n_groups : 3 * n_groups]
-    send, recv, local = rest[3 * n_groups :]
+def centroid_kernel(points, labels, old, all_points, blended, pts, lab, onehot, old_rows, weights, *rest):
+    n_chunks = len(WIDTHS)
+    parts, lands, cents, helds = (rest[k * n_chunks : (k + 1) * n_chunks] for k in range(4))
+    send, recv, local = rest[4 * n_chunks :]
     wires = Wires(send, recv, local)
     p, c = lax.axis_index("point"), lax.axis_index("cent")
     x, z, y, core = p // 4, lax.rem(p, 4), c // 2, lax.rem(c, 2)
@@ -138,12 +139,11 @@
     for load in loads:
         load.wait()
 
-    n_chunks = pts.shape[1] // LANES
     gathers = []
 
     def start_gather(t):
         if t < n_chunks:
-            block = lambda row, count: pts.at[pl.ds(row, count), pl.ds(t * LANES, LANES)]
+            block = lambda row, count: pts.at[pl.ds(row, count), pl.ds(STARTS[t], WIDTHS[t])]
             gathers.append(gather_chunk(wires, block, rows, up, down, sibling))
             next(gathers[t])
 
@@ -174,10 +174,10 @@
             count = jnp.dot(onehot[row, :], ones, preferred_element_type=F32).astype(jnp.int32)
             place = lax.broadcasted_iota(jnp.int32, count.shape, 1) & 3
             digit = lax.shift_right_logical(count, place * 4) & 15
-            parts[0][row, LANES:] = digit.astype(F32).astype(BF16)
+            parts[0][row, WIDTHS[0] :] = digit.astype(F32).astype(BF16)
 
     def finisher(g, half):
-        start, width = g * LANES, LANES
+        start, width = STARTS[g], WIDTHS[g]
 
         def finish(total):
             if g == 0:
@@ -197,24 +197,21 @@
     halves, stores = {}, []
 
     def sum_near(g):
+        lanes = slice(STARTS[g], STARTS[g] + WIDTHS[g])
+
         @pl.loop(0, n_rows // 256)
         def _(r):
             row = pl.ds(pl.multiple_of(r * 256, 256), 256)
-            held[row, :] = jnp.dot(
-                onehot[row, 0:near_rows], pts[0:near_rows, g * LANES : (g + 1) * LANES], preferred_element_type=F32
-            )
-
-    def reduce(g, split=False):
-        lanes = slice(g * LANES, (g + 1) * LANES)
+            helds[g][row, :] = jnp.dot(onehot[row, 0:near_rows], pts[0:near_rows, lanes], preferred_element_type=F32)
+
+    def reduce(g):
+        lanes = slice(STARTS[g], STARTS[g] + WIDTHS[g])
 
         @pl.loop(0, n_rows // 256)
         def _(r):
             row = pl.ds(pl.multiple_of(r * 256, 256), 256)
-            if split:
-                sums = held[row, :] + jnp.dot(onehot[row, near_rows:], pts[near_rows:, lanes], preferred_element_type=F32)
-            else:
-                sums = jnp.dot(onehot[row, :], pts[:, lanes], preferred_element_type=F32)
-            parts[g][row, 0:LANES] = sums.astype(BF16)
+            sums = jnp.dot(onehot[row, near_rows:], pts[near_rows:, lanes], preferred_element_type=F32)
+            parts[g][row, 0 : WIDTHS[g]] = (helds[g][row, :] + sums).astype(BF16)
 
         halves[g] = (
             reduce_half(wires, 0, x, z, x_ids, z_ids, parts[g], lands[g].at[0], cents[g], finisher(g, 0)),
@@ -231,11 +228,11 @@
         next(gathers[t])
 
     def store_points(t):
-        lanes = pl.ds(t * LANES, LANES)
+        lanes = pl.ds(STARTS[t], WIDTHS[t])
         stores.append(wires.here(pts.at[:, lanes], all_points.at[:, lanes]))
 
     def store_centroids(g):
-        stores.append(wires.here(cents[g], blended.at[:, pl.ds(g * LANES, LANES)]))
+        stores.append(wires.here(cents[g], blended.at[:, pl.ds(STARTS[g], WIDTHS[g])]))
 
     next(label_gather)
     next(label_gather)
@@ -243,46 +240,58 @@
     gathered(0)
     start_gather(2)
     match(range(4, 8))
+    gathered(0)
+    sum_near(0)
+    gathered(1)
+    start_gather(3)
     count_digits()
     for load in old_loads:
         load.wait()
     gathered(0)
     gathered(1)
-    start_gather(3)
-    gathered(0)
+    sum_near(1)
     gathered(0)
     reduce(0)
+    store_points(0)
+    gathered(2)
+    start_gather(4)
     gathered(1)
     gathered(2)
-    gathered(1)
+    sum_near(2)
     advance(0)
+    gathered(3)
     gathered(1)
     reduce(1)
+    store_points(1)
+    gathered(3)
+    sum_near(3)
+    gathered(2)
     advance(0)
-    gathered(2)
-    gathered(2)
-    gathered(3)
-    advance(0)
+    gathered(4)
     gathered(2)
     reduce(2)
-    for t in range(3):
-        store_points(t)
+    store_points(2)
+    advance(0)
+    gathered(3)
+    gathered(4)
+    sum_near(4)
     advance(1)
+    gathered(4)
     gathered(3)
-    sum_near(3)
-    gathered(3)
-    advance(1)
-    gathered(3)
-    reduce(3, split=True)
+    reduce(3)
+    gathered(4)
+    reduce(4)
     store_points(3)
-    advance(0, 1, 2, 3)
+    store_points(4)
+    advance(0)
     store_centroids(0)
-    advance(1, 2, 3)
+    advance(1, 2, 3, 4)
+    advance(1, 2, 3, 4)
+    advance(1, 2, 3, 4)
     store_centroids(1)
-    advance(2, 3)
-    advance(2, 3)
-    store_centroids(2)
-    store_centroids(3)
+    advance(2, 3, 4)
+    for g in (2, 3, 4):
+        store_centroids(g)
     for copy in wires.sent:
         copy.wait_send()
     for copy in stores:
@@ -330,8 +339,8 @@
     n_rows = old_centroids.shape[0]
     labels = jnp.broadcast_to(assign[None, :], (8, rows))
     group = 8 * rows
-    n_chunks = width // LANES
-    sums = [LANES + (DIGITS if g == 0 else 0) for g in range(n_chunks)]
+    n_chunks = len(WIDTHS)
+    sums = [w + (DIGITS if g == 0 else 0) for g, w in enumerate(WIDTHS)]
     n_remote = (6 + 24) * n_chunks + 8
     everywhere = pl.BlockSpec(memory_space=pl.ANY)
     all_points, blended = pl.pallas_call(
@@ -345,10 +354,10 @@
             pltpu.VMEM((n_rows, group), BF16),
             pltpu.VMEM((2, 32, width), BF16),
             pltpu.VMEM((2, 2, 32, 128), F32),
-            pltpu.VMEM((n_rows, LANES), F32),
             *[pltpu.VMEM((n_rows, w), BF16) for w in sums],
             *[pltpu.VMEM((2, 480, w), BF16) for w in sums],
-            *[pltpu.VMEM((n_rows, LANES), BF16) for _ in sums],
+            *[pltpu.VMEM((n_rows, w), BF16) for w in WIDTHS],
+            *[pltpu.VMEM((n_rows, w), F32) for w in WIDTHS],
             pltpu.SemaphoreType.DMA((n_remote,)),
             pltpu.SemaphoreType.DMA((n_remote,)),
             pltpu.SemaphoreType.DMA((4 + 2 * n_chunks,)),

time: 91.8 us -> 87.6 us (0.954)
  Pallas kernels: 89.7 us -> 85.5 us
    pallas_call x1, Pallas kernels: 75.9 us -> 71.7 us  [shards(): pl.pallas_call(centroid_kernel, out_shape=(jax.ShapeDtypeStruct((group, w...]
where the time goes in v4:
time: 87.6 us; the launch traced here: 87.5 us
  Pallas kernels  85.5 us (98%)
  local copies, waits for them, and re-layouts  1.29 us (1%)
    pallas_call x1, Pallas kernels, shards(): pl.pallas_call(centroid_kernel, out_shape=(jax.ShapeDtypeStruct((group, w...  71.7 us
    pallas_call x1, Pallas kernels, shards(): pl.pallas_call(distance_kernel, grid=(8,), out_shape=(jax.ShapeDtypeStruc...  13.9 us

profile of v4, /device:TPU:0, one launch (start us, length us, event | category | flops | bytes accessed | tf_op | source)
XLA Modules:
  0.0 87.5 jit_solution(7777614405532579893)
XLA Ops:
  0.6 1.3 %broadcast_in_dim.2.labels = s32[8,512]{1,0:T(8,128)} broadcast(s32[512]{0:T(512)} %param.4), dimensions={1} | broadcast | bytes 18432 | tf_op jit(solution)/shard_map/broadcast_in_dim | solution.py:340
  1.9 71.7 %shard_map.50 = (bf16[4096,1024]{1,0:T(8,128)(2,1)S(1)}, bf16[1024,1024]{1,0:T(8,128)(2,1)S(1)}) custom-call(bf16[512,1024]{1,0:T(8,128)(2,1)} %points.1, s32[8,512]{1,0:T(8,128)} %broadcast_in_dim.2.labels, bf16[1024,1024]{1,0:T(8,128)(2,1)} %old.1), custom_call_target="tpu_custom_call" | custom-call | flops 8589934592 | bytes 8388608 | tf_op jit(solution)/shard_map/pallas_call | solution.py:346
  73.6 13.9 %shard_map.51 = (bf16[1024,1024]{1,0:T(8,128)(2,1)}, f32[4096,1024]{1,0:T(8,128)}) custom-call(bf16[4096,1024]{1,0:T(8,128)(2,1)S(1)} %get-tuple-element.4.points, bf16[1024,1024]{1,0:T(8,128)(2,1)S(1)} %get-tuple-element.5.blended), custom_call_target="tpu_custom_call" | custom-call | flops 8589934592 | bytes 25165824 | tf_op jit(solution)/shard_map/pallas_call | solution.py:370

commit v5 on v4

v5 whole, which is shorter than its diff:
```python
import functools

import jax
import jax.numpy as jnp
from jax import lax
from jax.experimental import pallas as pl
from jax.experimental.pallas import tpu as pltpu
from jax.sharding import PartitionSpec as P

MESH = pl.DeviceIdType.MESH
F32, BF16 = jnp.float32, jnp.bfloat16
NT = (((1,), (1,)), ((), ()))
WIDTHS = (256, 256, 256, 256)
STARTS = tuple(sum(WIDTHS[:t]) for t in range(len(WIDTHS)))
GROUPS = ((0,), (1,), (2,), (3,))
SPANS = tuple((STARTS[g[0]], sum(WIDTHS[t] for t in g)) for g in GROUPS)
ROUTES = ((("x", 0, 32), ("z", 32, 32)),) * 4
EARLY = 512
DIGITS = 128


class Wires:
    def __init__(self, send, recv, local):
        self.send, self.recv, self.local = send, recv, local
        self.n_remote = self.n_local = 0
        self.sent = []

    def remote(self, src, dst, target):
        index = self.n_remote
        self.n_remote += 1
        copy = pltpu.make_async_remote_copy(
            src_ref=src, dst_ref=dst, send_sem=self.send.at[index], recv_sem=self.recv.at[index],
            device_id=target, device_id_type=MESH,
        )
        copy.start()
        self.sent.append(copy)
        return copy

    def settle(self, keep=0):
        count = max(len(self.sent) - keep, 0)
        for copy in self.sent[:count]:
            copy.wait_send()
        del self.sent[:count]

    def here(self, src, dst):
        copy = pltpu.make_async_copy(src, dst, self.local.at[self.n_local])
        self.n_local += 1
        copy.start()
        return copy


def gather_chunk(wires, block, rows, up, down, sibling):
    half = rows // 2
    from_below = wires.remote(block(0, rows), block(rows, rows), up)
    from_above = wires.remote(block(0, rows), block(2 * rows, rows), down)
    yield
    from_below.wait_recv()
    far_a = wires.remote(block(rows, half), block(6 * rows, half), up)
    from_above.wait_recv()
    far_b = wires.remote(block(2 * rows + half, half), block(6 * rows + half, half), down)
    near = wires.remote(block(0, 3 * rows), block(3 * rows, 3 * rows), sibling)
    yield
    near.wait_recv()
    yield
    far_a.wait_recv()
    far_b.wait_recv()
    far = wires.remote(block(6 * rows, rows), block(7 * rows, rows), sibling)
    yield
    far.wait_recv()
    yield


def gather_labels(wires, lab, up, down, across, sibling):
    first = [wires.remote(lab.at[0], lab.at[k], target) for k, target in ((6, across), (1, up), (2, down))]
    near = [wires.remote(lab.at[0], lab.at[3], sibling)]
    yield
    for copy, k, to in zip(first[1:] + first[:1], (1, 2, 6), (4, 5, 7)):
        copy.wait_recv()
        near.append(wires.remote(lab.at[k], lab.at[to], sibling))
    yield
    for copy in near:
        copy.wait_recv()
    yield


def add(*terms):
    total = terms[0].astype(F32)
    for term in terms[1:]:
        total = total + term.astype(F32)
    return total


def reduce_rows(wires, x_first, low, size, x, z, x_ids, z_ids, part, cent, land, land_two, finish):
    order = (2, 1, 3)
    rows = pl.ds(low, size)
    first_ids, second_ids = (x_ids, z_ids) if x_first else (z_ids, x_ids)

    def block(k):
        return (lax.rem(x + k, 4), slice(None), rows) if x_first else (slice(None), lax.rem(z + k, 4), rows)

    def cell(k):
        return (x, lax.rem(z + k, 4), rows) if x_first else (lax.rem(x + k, 4), z, rows)

    copies = [wires.remote(part.at[block(k)], land.at[k - 1], first_ids[k]) for k in order]
    yield
    for copy in copies:
        copy.wait_recv()
    part[block(0)] = add(part[block(0)], land[0], land[1], land[2]).astype(BF16)
    copies = [wires.remote(part.at[cell(k)], land_two.at[k - 1], second_ids[k]) for k in order]
    yield
    for copy in copies:
        copy.wait_recv()
    cent[cell(0)] = finish(add(part[cell(0)], land_two[0], land_two[1], land_two[2]))
    copies = [wires.remote(cent.at[cell(0)], cent.at[cell(0)], second_ids[k]) for k in order]
    yield
    for copy in copies:
        copy.wait_recv()
    copies = [wires.remote(cent.at[block(0)], cent.at[block(0)], first_ids[k]) for k in order]
    yield
    for copy in copies:
        copy.wait_recv()
    yield


def centroid_kernel(points, labels, old, products_a, products_b, products_c, products_d, late_points, blended, point_sq, pts, lab, onehot, old_rows, weights, cents, *rest):
    n_chunks, n_groups = len(WIDTHS), len(GROUPS)
    n_routes = sum(len(routes) for routes in ROUTES)
    parts, rest = rest[:n_groups], rest[n_groups:]
    lands, lands_two, rest = rest[:n_routes], rest[n_routes : 2 * n_routes], rest[2 * n_routes :]
    held_a, held_b, send, recv, local = rest
    helds = [(held_a, held_b)[t % 2].at[:, pl.ds(0, w)] for t, w in enumerate(WIDTHS)]
    wires = Wires(send, recv, local)
    p, c = lax.axis_index("point"), lax.axis_index("cent")
    x, z, y, core = p // 4, lax.rem(p, 4), c // 2, lax.rem(c, 2)

    def ring(k, by):
        return lax.rem(k + 4 + by, 4)

    up, across, down = ({"cent": ring(y, by) * 2 + core} for by in (1, 2, 3))
    sibling = {"cent": y * 2 + 1 - core}
    x_ids = {by: {"point": ring(x, by) * 4 + z} for by in (1, 2, 3)}
    z_ids = {by: {"point": x * 4 + ring(z, by)} for by in (1, 2, 3)}
    partners = (up, across, down, sibling, *x_ids.values(), *z_ids.values())

    rows = points.shape[0]
    loads = [wires.here(labels, lab.at[0]), wires.here(points, pts.at[pl.ds(0, rows)])]
    old_load = wires.here(old.at[pl.ds(pl.multiple_of(p * 64, 64), 64)], old_rows)

    barrier = pltpu.get_barrier_semaphore()
    for other in partners:
        pl.semaphore_signal(barrier, inc=1, device_id=other, device_id_type=MESH)
    pl.semaphore_wait(barrier, len(partners))
    for load in loads:
        load.wait()

    gathers = []

    def start_gather(t):
        if t < n_chunks:
            block = lambda row, count: pts.at[pl.ds(row, count), pl.ds(STARTS[t], WIDTHS[t])]
            gathers.append(gather_chunk(wires, block, rows, up, down, sibling))
            next(gathers[t])

    label_gather = gather_labels(wires, lab, up, down, across, sibling)
    next(label_gather)
    start_gather(0)
    start_gather(1)

    n_rows = onehot.shape[0]
    first_id = c * n_rows
    tile = 64

    def match(slots):
        @pl.loop(0, n_rows // tile)
        def _(r):
            row = pl.multiple_of(r * tile, tile)
            ids = first_id + row + lax.broadcasted_iota(jnp.int32, (tile, rows), 0)
            for k in slots:
                same = ids == lab[k, 0:1, :]
                onehot[pl.ds(row, tile), k * rows : (k + 1) * rows] = jnp.where(same, 1.0, 0.0).astype(BF16)

    def count_digits():
        ones = jnp.ones((onehot.shape[1], DIGITS), BF16)

        @pl.loop(0, 4)
        def _(r):
            row = pl.ds(pl.multiple_of(r * 256, 256), 256)
            count = jnp.dot(onehot[row, :], ones, preferred_element_type=F32).astype(jnp.int32)
            place = lax.broadcasted_iota(jnp.int32, count.shape, 1) & 3
            digit = lax.shift_right_logical(count, place * 4) & 15
            parts[0][r, :, :, SPANS[0][1] :] = digit.astype(F32).astype(BF16).reshape(4, 64, DIGITS)

    def finisher(g, low, size):
        start, width = SPANS[g]
        mine = slice(low, low + size)

        def finish(total):
            if g == 0:
                place = lax.broadcasted_iota(jnp.int32, (size, DIGITS), 1)
                scale = jnp.where(place == 0, 1.0, jnp.where(place == 1, 16.0, jnp.where(place == 2, 256.0, 4096.0)))
                digits = jnp.where(place < 4, total[:, width:] * scale, 0.0)
                count = jnp.sum(digits, axis=1, keepdims=True)
                weights[0, mine] = jnp.broadcast_to(jnp.where(count > 0.0, 0.5 / jnp.maximum(count, 1.0), 0.0), (size, 128))
                weights[1, mine] = jnp.broadcast_to(jnp.where(count > 0.0, 0.5, 1.0), (size, 128))
            old_part = old_rows[mine, start : start + width].astype(F32)
            return (total[:, :width] * weights[0, mine, 0:1] + old_part * weights[1, mine, 0:1]).astype(BF16)

        return finish

    near_rows = 6 * rows
    routes_of, stores = {}, []

    def sum_near(t):
        lanes = slice(STARTS[t], STARTS[t] + WIDTHS[t])

        @pl.loop(0, n_rows // 256)
        def _(r):
            row = pl.ds(pl.multiple_of(r * 256, 256), 256)
            helds[t][row, :] = jnp.dot(onehot[row, 0:near_rows], pts[0:near_rows, lanes], preferred_element_type=F32)

    def sum_far(t):
        lanes = slice(STARTS[t], STARTS[t] + WIDTHS[t])
        g = [t in group for group in GROUPS].index(True)
        to = slice(STARTS[t] - SPANS[g][0], STARTS[t] - SPANS[g][0] + WIDTHS[t])

        @pl.loop(0, 4)
        def _(r):
            row = pl.ds(pl.multiple_of(r * 256, 256), 256)
            sums = jnp.dot(onehot[row, near_rows:], pts[near_rows:, lanes], preferred_element_type=F32)
            parts[g][r, :, :, to] = (helds[t][row, :] + sums).astype(BF16).reshape(4, 64, WIDTHS[t])

    def reduce(g):
        cent = cents.at[:, :, :, pl.ds(*SPANS[g])]
        begin = sum(len(routes) for routes in ROUTES[:g])
        routes_of[g] = [
            reduce_rows(
                wires, axis == "x", low, size, x, z, x_ids, z_ids,
                parts[g], cent, lands[begin + i], lands_two[begin + i], finisher(g, low, size),
            )
            for i, (axis, low, size) in enumerate(ROUTES[g])
        ]
        advance(g)

    def advance(*groups):
        for g in groups:
            for route in routes_of[g]:
                next(route)

    def gathered(t):
        next(gathers[t])

    def store_points(t):
        if STARTS[t] >= EARLY:
            to = pl.ds(STARTS[t] - EARLY, WIDTHS[t])
            stores.append(wires.here(pts.at[:, pl.ds(STARTS[t], WIDTHS[t])], late_points.at[:, to]))

    def store_centroids(g):
        lanes = pl.ds(*SPANS[g])
        stores.append(wires.here(cents.at[:, :, :, lanes], blended.at[:, :, :, lanes]))

    def square_points():
        @pl.loop(0, pts.shape[0] // 256)
        def _(r):
            row = pl.ds(pl.multiple_of(r * 256, 256), 256)
            wide = pts[row, :].astype(F32)
            point_sq[row, :] = jnp.broadcast_to(jnp.sum(wide * wide, axis=1, keepdims=True), (256, point_sq.shape[1]))

    def multiply_early():
        for k, products in enumerate((products_a, products_b, products_c, products_d)):

            @pl.loop(0, 2)
            def _(r):
                row = pl.ds(pl.multiple_of(2 * k * rows + r * rows, rows), rows)
                rhs = cents[:, :, :, 0:EARLY].reshape(n_rows, EARLY)
                products[pl.ds(pl.multiple_of(r * rows, rows), rows), :] = lax.dot_general(
                    pts[row, 0:EARLY], rhs, NT, preferred_element_type=F32
                )

    next(label_gather)
    next(label_gather)
    match(range(4))
    gathered(0)
    start_gather(2)
    match(range(4, 8))
    gathered(0)
    sum_near(0)
    gathered(1)
    start_gather(3)
    count_digits()
    old_load.wait()
    gathered(0)
    gathered(1)
    sum_near(1)
    gathered(0)
    sum_far(0)
    reduce(0)
    gathered(2)
    gathered(1)
    gathered(2)
    sum_near(2)
    gathered(1)
    sum_far(1)
    reduce(1)
    advance(0)
    gathered(2)
    gathered(3)
    gathered(2)
    sum_far(2)
    reduce(2)
    advance(0)
    gathered(3)
    sum_near(3)
    gathered(3)
    advance(1)
    gathered(3)
    sum_far(3)
    reduce(3)
    advance(0)
    store_points(2)
    store_points(3)
    square_points()
    advance(1)
    advance(2)
    advance(3)
    advance(0)
    store_centroids(0)
    advance(1)
    advance(2)
    advance(3)
    wires.settle(20)
    advance(2)
    advance(1)
    store_centroids(1)
    advance(3)
    wires.settle(12)
    multiply_early()
    advance(2)
    store_centroids(2)
    advance(3)
    store_centroids(3)
    wires.settle()
    for copy in stores:
        copy.wait()


def distance_kernel(products_a, products_b, products_c, products_d, points, blended, point_sq, new, out, made, rows_of, staged, sems):
    n_rows, group, block = made.shape[0], points.shape[0], staged.shape[1]
    flat = blended.reshape(n_rows, blended.shape[3])
    tile = 128
    for r in range(n_rows // tile):
        row = pl.ds(r * tile, tile)
        wide = flat[row, :].astype(F32)
        scale = lax.rsqrt(jnp.sum(wide * wide, axis=1, keepdims=True) + 1e-06)
        rounded = (wide * scale).astype(BF16)
        made[row, :] = rounded
        square = jnp.square(rounded.astype(F32))
        cent_sq = jnp.sum(square, axis=1, keepdims=True)
        lane = lax.broadcasted_iota(jnp.int32, (tile, 128), 1)
        rows_of[:, r * tile : (r + 1) * tile] = jnp.where(lane < 8, scale, cent_sq).T
    new_copy = pltpu.make_async_copy(made, new, sems.at[staged.shape[0]])
    new_copy.start()
    twice, cent_sq = 2.0 * rows_of[0:1, :], rows_of[8:9, :]

    c = lax.axis_index("cent")
    y, core = c // 2, lax.rem(c, 2)
    copies = []
    for k in range(group // block):
        shift = 2 if k >= 6 else (0, 3, 1)[k % 3]
        side = 1 - core if k in (3, 4, 5, 7) else core
        place = (lax.rem(y + shift, 4) * 2 + side) * block
        slot = k % staged.shape[0]
        if k >= staged.shape[0]:
            copies[k - staged.shape[0]].wait()
        row = slice(k * block, (k + 1) * block)
        early = (products_a, products_b, products_c, products_d)[k // 2][(k % 2) * block : (k % 2 + 1) * block, :]
        late = lax.dot_general(points[row, :], flat[:, EARLY:], NT, preferred_element_type=F32)
        staged[slot] = (point_sq[row, 0:1] + cent_sq) - twice * (early + late)
        copies.append(pltpu.make_async_copy(staged.at[slot], out.at[pl.ds(pl.multiple_of(place, block), block)], sems.at[slot]))
        copies[-1].start()
    for copy in copies[-staged.shape[0] :]:
        copy.wait()
    new_copy.wait()


def shards(points, assign, old_centroids):
    rows, width = points.shape
    n_rows = old_centroids.shape[0]
    labels = jnp.broadcast_to(assign[None, :], (8, rows))
    group = 8 * rows
    n_chunks = len(WIDTHS)
    sums = [w + (DIGITS if g == 0 else 0) for g, (_, w) in enumerate(SPANS)]
    routes = [(size, sums[g]) for g, of_group in enumerate(ROUTES) for _, _, size in of_group]
    n_remote = 6 * n_chunks + 12 * len(routes) + 8
    hbm, vmem = pl.BlockSpec(memory_space=pltpu.HBM), pl.BlockSpec(memory_space=pltpu.VMEM)
    handed_on = pl.pallas_call(
        centroid_kernel,
        out_shape=(
            *[pltpu.VMEM((group // 4, n_rows), F32)] * 4,
            pltpu.VMEM((group, width - EARLY), BF16),
            pltpu.VMEM((4, 4, 64, width), BF16),
            pltpu.VMEM((group, 128), F32),
        ),
        in_specs=[hbm] * 3,
        out_specs=(vmem,) * 7,
        scratch_shapes=[
            pltpu.VMEM((group, width), BF16),
            pltpu.VMEM((8, 8, rows), jnp.int32),
            pltpu.VMEM((n_rows, group), BF16),
            pltpu.VMEM((64, width), BF16),
            pltpu.VMEM((2, 64, 128), F32),
            pltpu.VMEM((4, 4, 64, width), BF16),
            *[pltpu.VMEM((4, 4, 64, w), BF16) for w in sums],
            *[pltpu.VMEM((3, 4, size, w), BF16) for size, w in routes],
            *[pltpu.VMEM((3, size, w), BF16) for size, w in routes],
            *[pltpu.VMEM((n_rows, max(WIDTHS)), F32)] * 2,
            pltpu.SemaphoreType.DMA((n_remote,)),
            pltpu.SemaphoreType.DMA((n_remote,)),
            pltpu.SemaphoreType.DMA((4 + 2 * n_chunks,)),
        ],
        compiler_params=pltpu.CompilerParams(
            collective_id=0, has_side_effects=True, vmem_limit_bytes=26 * 2**20
        ),
        cost_estimate=pl.CostEstimate(flops=3 * n_rows * group * width, bytes_accessed=2 * group * width, transcendentals=0),
    )(*(pltpu.with_memory_space_constraint(a, pltpu.HBM) for a in (points, labels, old_centroids)))
    new_centroids, distances = pl.pallas_call(
        distance_kernel,
        out_shape=(jax.ShapeDtypeStruct((n_rows, width), BF16), jax.ShapeDtypeStruct((group, n_rows), F32)),
        in_specs=[vmem] * 7,
        out_specs=(hbm, hbm),
        scratch_shapes=[
            pltpu.VMEM((n_rows, width), BF16),
            pltpu.VMEM((128, n_rows), F32),
            pltpu.VMEM((3, rows, n_rows), F32),
            pltpu.SemaphoreType.DMA((4,)),
        ],
        compiler_params=pltpu.CompilerParams(vmem_limit_bytes=16 * 2**20),
        cost_estimate=pl.CostEstimate(flops=n_rows * group * width, bytes_accessed=4 * group * n_rows, transcendentals=0),
    )(*(pltpu.with_memory_space_constraint(a, pltpu.VMEM) for a in handed_on))
    return new_centroids, distances


def solution(mesh):
    return jax.shard_map(
        shards,
        mesh=mesh,
        in_specs=(P(("point", "cent"), None), P(("point", "cent")), P("cent", None)),
        out_specs=(P("cent", None), P("point", "cent")),
        check_vma=False,
    )
```

time: 87.6 us -> 83.3 us (0.951)
  Pallas kernels: 85.5 us -> 81.1 us
    pallas_call x2, Pallas kernels: 85.5 us -> 81.1 us  [the longest x1 72.4 us: shards(): pl.pallas_call(centroid_kernel, out_shape=(*[pltpu.VMEM((group // 4, n_ro...]
where the time goes in v5:
time: 83.3 us; the launch traced here: 83.2 us
  Pallas kernels  81.1 us (97%)
  local copies, waits for them, and re-layouts  1.29 us (2%)
    pallas_call x1, Pallas kernels, shards(): pl.pallas_call(centroid_kernel, out_shape=(*[pltpu.VMEM((group // 4, n_ro...  72.4 us
    pallas_call x1, Pallas kernels, shards(): pl.pallas_call(distance_kernel, out_shape=(jax.ShapeDtypeStruct((n_rows,...  8.71 us

profile of v5, /device:TPU:0, one launch (start us, length us, event | category | flops | bytes accessed | tf_op | source)
XLA Modules:
  0.0 83.2 jit_solution(7495720887986050478)
XLA Ops:
  0.6 1.3 %broadcast_in_dim.2.labels = s32[8,512]{1,0:T(8,128)} broadcast(s32[512]{0:T(512)} %param.4), dimensions={1} | broadcast | bytes 18432 | tf_op jit(solution)/shard_map/broadcast_in_dim | solution.py:388
  1.9 72.4 %shard_map.50 = (f32[1024,1024]{1,0:T(8,128)S(1)}, f32[1024,1024]{1,0:T(8,128)S(1)}, f32[1024,1024]{1,0:T(8,128)S(1)}, f32[1024,1024]{1,0:T(8,128)S(1)}, bf16[40...) custom-call(bf16[512,1024]{1,0:T(8,128)(2,1)} %points.1, ...), custom_call_target="tpu_custom_call" | custom-call | flops 12884901888 | bytes 8388608 | tf_op jit(solution)/shard_map/pallas_call | solution.py:395
  74.3 8.7 %shard_map.51 = (bf16[1024,1024]{1,0:T(8,128)(2,1)}, f32[4096,1024]{1,0:T(8,128)}) custom-call(f32[1024,1024]{1,0:T(8,128)S(1)} %get-tuple-element.9.products_a, f32[1024,1024]{1,0:T(8,128)S(1)} %get-tuple-element.10.products_b, f32[1024,1024]{1,0:T(8,128)S(1)} %get-tuple-element.11.products_c, f32[1024,1024]{1,0:T(8,128)S(1)} %get-tuple-element.12.products_d, ...), custom_call_target="tpu_custom_call" | custom-call | flops 4294967296 | bytes 16777216 | tf_op jit(solution)/shard_map/pallas_call | solution.py:425

commit v6 on v5

--- a/solution.py
+++ b/solution.py
@@ -176,7 +176,7 @@
             row = pl.multiple_of(r * tile, tile)
             ids = first_id + row + lax.broadcasted_iota(jnp.int32, (tile, rows), 0)
             for k in slots:
-                same = ids == lab[k, 0:1, :]
+                same = ids == lab[k]
                 onehot[pl.ds(row, tile), k * rows : (k + 1) * rows] = jnp.where(same, 1.0, 0.0).astype(BF16)
 
     def count_digits():
@@ -301,9 +301,9 @@
     gathered(1)
     sum_far(1)
     reduce(1)
+    gathered(3)
     advance(0)
     gathered(2)
-    gathered(3)
     gathered(2)
     sum_far(2)
     reduce(2)
@@ -385,7 +385,7 @@
 def shards(points, assign, old_centroids):
     rows, width = points.shape
     n_rows = old_centroids.shape[0]
-    labels = jnp.broadcast_to(assign[None, :], (8, rows))
+    labels = assign.reshape(1, rows)
     group = 8 * rows
     n_chunks = len(WIDTHS)
     sums = [w + (DIGITS if g == 0 else 0) for g, (_, w) in enumerate(SPANS)]
@@ -404,7 +404,7 @@
         out_specs=(vmem,) * 7,
         scratch_shapes=[
             pltpu.VMEM((group, width), BF16),
-            pltpu.VMEM((8, 8, rows), jnp.int32),
+            pltpu.VMEM((8, 1, rows), jnp.int32),
             pltpu.VMEM((n_rows, group), BF16),
             pltpu.VMEM((64, width), BF16),
             pltpu.VMEM((2, 64, 128), F32),

time: 83.3 us -> 81.4 us (0.977)
  local copies, waits for them, and re-layouts: 1.29 us -> 0 us
    broadcast_in_dim x1 -> x0, local copies, waits for them, and re-layouts: 1.29 us -> none  [shards(): labels = jnp.broadcast_to(assign[None, :], (8, rows))]
where the time goes in v6:
time: 81.4 us; the launch traced here: 81.3 us
  Pallas kernels  80.5 us (99%)
    pallas_call x1, Pallas kernels, shards(): pl.pallas_call(centroid_kernel, out_shape=(*[pltpu.VMEM((group // 4, n_ro...  71.8 us
    pallas_call x1, Pallas kernels, shards(): pl.pallas_call(distance_kernel, out_shape=(jax.ShapeDtypeStruct((n_rows,...  8.71 us

profile of v6, /device:TPU:0, one launch (start us, length us, event | category | flops | bytes accessed | tf_op | source)
XLA Modules:
  0.0 81.3 jit_solution(7392215867817730847)
XLA Ops:
  0.6 71.8 %shard_map.50 = (f32[1024,1024]{1,0:T(8,128)S(1)}, f32[1024,1024]{1,0:T(8,128)S(1)}, f32[1024,1024]{1,0:T(8,128)S(1)}, f32[1024,1024]{1,0:T(8,128)S(1)}, bf16[40...) custom-call(bf16[512,1024]{1,0:T(8,128)(2,1)} %points.1, s32[1,512]{1,0:T(1,128)} %bitcast.1, ...), custom_call_target="tpu_custom_call" | custom-call | flops 12884901888 | bytes 8388608 | tf_op jit(solution)/shard_map/pallas_call | solution.py:395
  72.4 8.7 %shard_map.51 = (bf16[1024,1024]{1,0:T(8,128)(2,1)}, f32[4096,1024]{1,0:T(8,128)}) custom-call(f32[1024,1024]{1,0:T(8,128)S(1)} %get-tuple-element.9.products_a, f32[1024,1024]{1,0:T(8,128)S(1)} %get-tuple-element.10.products_b, f32[1024,1024]{1,0:T(8,128)S(1)} %get-tuple-element.11.products_c, f32[1024,1024]{1,0:T(8,128)S(1)} %get-tuple-element.12.products_d, ...), custom_call_target="tpu_custom_call" | custom-call | flops 4294967296 | bytes 16777216 | tf_op jit(solution)/shard_map/pallas_call | solution.py:425

commit v7 on v6

--- a/solution.py
+++ b/solution.py
@@ -357,7 +357,7 @@
         cent_sq = jnp.sum(square, axis=1, keepdims=True)
         lane = lax.broadcasted_iota(jnp.int32, (tile, 128), 1)
         rows_of[:, r * tile : (r + 1) * tile] = jnp.where(lane < 8, scale, cent_sq).T
-    new_copy = pltpu.make_async_copy(made, new, sems.at[staged.shape[0]])
+    new_copy = pltpu.make_async_copy(made, new, sems.at[0])
     new_copy.start()
     twice, cent_sq = 2.0 * rows_of[0:1, :], rows_of[8:9, :]
 
@@ -370,15 +370,22 @@
         place = (lax.rem(y + shift, 4) * 2 + side) * block
         slot = k % staged.shape[0]
         if k >= staged.shape[0]:
-            copies[k - staged.shape[0]].wait()
-        row = slice(k * block, (k + 1) * block)
-        early = (products_a, products_b, products_c, products_d)[k // 2][(k % 2) * block : (k % 2 + 1) * block, :]
-        late = lax.dot_general(points[row, :], flat[:, EARLY:], NT, preferred_element_type=F32)
-        staged[slot] = (point_sq[row, 0:1] + cent_sq) - twice * (early + late)
-        copies.append(pltpu.make_async_copy(staged.at[slot], out.at[pl.ds(pl.multiple_of(place, block), block)], sems.at[slot]))
-        copies[-1].start()
-    for copy in copies[-staged.shape[0] :]:
-        copy.wait()
+            for copy in copies[k - staged.shape[0]]:
+                copy.wait()
+        copies.append([])
+        for q in range(2):
+            piece = block // 2
+            row = slice(k * block + q * piece, k * block + (q + 1) * piece)
+            begin = (k % 2) * block + q * piece
+            early = (products_a, products_b, products_c, products_d)[k // 2][begin : begin + piece, :]
+            late = lax.dot_general(points[row, :], flat[:, EARLY:], NT, preferred_element_type=F32)
+            staged[slot, q * piece : (q + 1) * piece] = (point_sq[row, 0:1] + cent_sq) - twice * (early + late)
+            to = out.at[pl.ds(pl.multiple_of(place + q * piece, piece), piece)]
+            copies[-1].append(pltpu.make_async_copy(staged.at[slot, pl.ds(q * piece, piece)], to, sems.at[1 + 4 * slot + q]))
+            copies[-1][-1].start()
+    for pieces in copies[-staged.shape[0] :]:
+        for copy in pieces:
+            copy.wait()
     new_copy.wait()
 
 
@@ -431,7 +438,7 @@
             pltpu.VMEM((n_rows, width), BF16),
             pltpu.VMEM((128, n_rows), F32),
             pltpu.VMEM((3, rows, n_rows), F32),
-            pltpu.SemaphoreType.DMA((4,)),
+            pltpu.SemaphoreType.DMA((13,)),
         ],
         compiler_params=pltpu.CompilerParams(vmem_limit_bytes=16 * 2**20),
         cost_estimate=pl.CostEstimate(flops=n_rows * group * width, bytes_accessed=4 * group * n_rows, transcendentals=0),

time: 81.4 us -> 81.3 us (level)
  no operation moved by 1% of the time
where the time goes in v7:
time: 81.3 us; the launch traced here: 81.2 us
  Pallas kernels  80.4 us (99%)
    pallas_call x1, Pallas kernels, shards(): pl.pallas_call(centroid_kernel, out_shape=(*[pltpu.VMEM((group // 4, n_ro...  71.8 us
    pallas_call x1, Pallas kernels, shards(): pl.pallas_call(distance_kernel, out_shape=(jax.ShapeDtypeStruct((n_rows,...  8.64 us

profile of v7, /device:TPU:0, one launch (start us, length us, event | category | flops | bytes accessed | tf_op | source)
XLA Modules:
  0.0 81.2 jit_solution(7106809022226427007)
XLA Ops:
  0.6 71.8 %shard_map.50 = (f32[1024,1024]{1,0:T(8,128)S(1)}, f32[1024,1024]{1,0:T(8,128)S(1)}, f32[1024,1024]{1,0:T(8,128)S(1)}, f32[1024,1024]{1,0:T(8,128)S(1)}, bf16[40...) custom-call(bf16[512,1024]{1,0:T(8,128)(2,1)} %points.1, s32[1,512]{1,0:T(1,128)} %bitcast.1, ...), custom_call_target="tpu_custom_call" | custom-call | flops 12884901888 | bytes 8388608 | tf_op jit(solution)/shard_map/pallas_call | solution.py:402
  72.4 8.6 %shard_map.51 = (bf16[1024,1024]{1,0:T(8,128)(2,1)}, f32[4096,1024]{1,0:T(8,128)}) custom-call(f32[1024,1024]{1,0:T(8,128)S(1)} %get-tuple-element.9.products_a, f32[1024,1024]{1,0:T(8,128)S(1)} %get-tuple-element.10.products_b, f32[1024,1024]{1,0:T(8,128)S(1)} %get-tuple-element.11.products_c, f32[1024,1024]{1,0:T(8,128)S(1)} %get-tuple-element.12.products_d, ...), custom_call_target="tpu_custom_call" | custom-call | flops 4294967296 | bytes 16777216 | tf_op jit(solution)/shard_map/pallas_call | solution.py:432

commit v8 on v7

--- a/solution.py
+++ b/solution.py
@@ -162,8 +162,8 @@
             next(gathers[t])
 
     label_gather = gather_labels(wires, lab, up, down, across, sibling)
+    start_gather(0)
     next(label_gather)
-    start_gather(0)
     start_gather(1)
 
     n_rows = onehot.shape[0]

time: 81.3 us -> 82.5 us (1.015)
  Pallas kernels: 80.4 us -> 81.3 us
    pallas_call x1, Pallas kernels: 71.8 us -> 72.6 us  [shards(): pl.pallas_call(centroid_kernel, out_shape=(*[pltpu.VMEM((group // 4, n_ro...]
where the time goes in v8:
time: 82.5 us; the launch traced here: 82.1 us
  Pallas kernels  81.3 us (99%)
    pallas_call x1, Pallas kernels, shards(): pl.pallas_call(centroid_kernel, out_shape=(*[pltpu.VMEM((group // 4, n_ro...  72.6 us
    pallas_call x1, Pallas kernels, shards(): pl.pallas_call(distance_kernel, out_shape=(jax.ShapeDtypeStruct((n_rows,...  8.65 us

profile of v8, /device:TPU:0, one launch (start us, length us, event | category | flops | bytes accessed | tf_op | source)
XLA Modules:
  0.0 82.1 jit_solution(10147457731564986651)
XLA Ops:
  0.6 72.6 %shard_map.50 = (f32[1024,1024]{1,0:T(8,128)S(1)}, f32[1024,1024]{1,0:T(8,128)S(1)}, f32[1024,1024]{1,0:T(8,128)S(1)}, f32[1024,1024]{1,0:T(8,128)S(1)}, bf16[40...) custom-call(bf16[512,1024]{1,0:T(8,128)(2,1)} %points.1, s32[1,512]{1,0:T(1,128)} %bitcast.1, ...), custom_call_target="tpu_custom_call" | custom-call | flops 12884901888 | bytes 8388608 | tf_op jit(solution)/shard_map/pallas_call | solution.py:402
  73.3 8.6 %shard_map.51 = (bf16[1024,1024]{1,0:T(8,128)(2,1)}, f32[4096,1024]{1,0:T(8,128)}) custom-call(f32[1024,1024]{1,0:T(8,128)S(1)} %get-tuple-element.9.products_a, f32[1024,1024]{1,0:T(8,128)S(1)} %get-tuple-element.10.products_b, f32[1024,1024]{1,0:T(8,128)S(1)} %get-tuple-element.11.products_c, f32[1024,1024]{1,0:T(8,128)S(1)} %get-tuple-element.12.products_d, ...), custom_call_target="tpu_custom_call" | custom-call | flops 4294967296 | bytes 16777216 | tf_op jit(solution)/shard_map/pallas_call | solution.py:432
